TPU v7x, 32 devices: a whole 2x2x4 slice. The times are simulated.
32 devices in a mesh: seq: 8 (over z, x), head: 4 (over y, core).
Axes of the slice: x: 2, y: 2, z: 4, core: 2. Of those that a mesh axis runs over, the one named last changes fastest.
Arguments:
- inputs: bfloat16 [8, 2048, 768], P(None, 'seq'), may hold values from -6 to 6
- lengths: int32 [8], replicated, may hold values from 512 to 2048, as said below
- norm_gain: float32 [768], replicated, may hold values from 0.5 to 1.5
- in_proj: float32 [768, 3352], P(None, 'head'), may hold values from -0.21875 to 0.21875
- conv_weight: float32 [4, 1792], P(None, 'head'), may hold values from -3 to 3
- conv_bias: float32 [1792], P('head'), may hold values from -1.75 to 1.75
- head_params: float32 [3, 24], P(None, 'head'), may hold values from -9.2 to 1.5, as said below
- gate_gain: float32 [1536], P('head'), may hold values from 0.5 to 1.5
- out_proj: float32 [1536, 768], P('head'), may hold values from -0.15625 to 0.15625
- cotangent: bfloat16 [8, 2048, 768], P(None, 'seq'), may hold values from -6 to 6
- norm_gain_mom: float32 [768], replicated, may hold values from -384 to 384
- in_proj_mom: float32 [768, 3352], P('seq', 'head'), may hold values from -192 to 192
- conv_weight_mom: float32 [4, 1792], P(None, 'head'), may hold values from -384 to 384
- conv_bias_mom: float32 [1792], P('head'), may hold values from -384 to 384
- head_params_mom: float32 [3, 24], P(None, 'head'), may hold values from -384 to 384
- gate_gain_mom: float32 [1536], P('head'), may hold values from -384 to 384
- out_proj_mom: float32 [1536, 768], P('head', 'seq'), may hold values from -640 to 640
Outputs:
- output: bfloat16 [8, 2048, 768], P(None, 'seq')
- input_grad: float32 [8, 2048, 768], P(None, 'seq')
- norm_gain_grad: float32 [768], replicated
- in_proj_grad: float32 [768, 3352], P('seq', 'head')
- conv_weight_grad: float32 [4, 1792], P(None, 'head')
- conv_bias_grad: float32 [1792], P('head')
- head_params_grad: float32 [3, 24], P(None, 'head')
- gate_gain_grad: float32 [1536], P('head')
- out_proj_grad: float32 [1536, 768], P('head', 'seq')
- norm_gain_mom_new: float32 [768], replicated
- in_proj_mom_new: float32 [768, 3352], P('seq', 'head')
- conv_weight_mom_new: float32 [4, 1792], P(None, 'head')
- conv_bias_mom_new: float32 [1792], P('head')
- head_params_mom_new: float32 [3, 24], P(None, 'head')
- gate_gain_mom_new: float32 [1536], P('head')
- out_proj_mom_new: float32 [1536, 768], P('head', 'seq')
- norm_gain_new: float32 [768], replicated
- in_proj_new: float32 [768, 3352], P('seq', 'head')
- conv_weight_new: float32 [4, 1792], P(None, 'head')
- conv_bias_new: float32 [1792], P('head')
- head_params_new: float32 [3, 24], P(None, 'head')
- gate_gain_new: float32 [1536], P('head')
- out_proj_new: float32 [1536, 768], P('head', 'seq')
- rms: float32 [], replicated
Inputs may be any that keep to these rules, and one draw needn't show every extreme that they name: `lengths`: each length lies between 512 and 2048; one sequence, which one drawn from the seed, fills all 2048 slots. `head_params`: row 0 holds dt biases, row 1 logarithms of decay rates, row 2 skip weights.
All inputs are finite; a program needn't handle non-finite values.
Results may differ from a plain program's by a relative error of at most 0.0083.
The roundings to bfloat16 on the way count: a program that leaves them out, or rounds other values in their place, can miss the bound.
Values may be sent and summed in bfloat16 or wider, within the bound.
No kernel may reach another device: no remote copies, remote signals or barrier semaphores. Data moves between devices by JAX's collectives and lax.ppermute only.
A program may use at most 448 MiB of HBM per device.

v0:
```python
import math

import jax
import jax.numpy as jnp
from jax import lax
from jax.sharding import PartitionSpec as P

NS_STEPS = 5


EPSILON = 1e-05
COEF_A = 3.4445
COEF_B = -4.775
COEF_C = 2.0315
MUON_RATE = 0.2
SMALL_RATE = 0.2
PRECISE = lax.Precision.HIGHEST


def shifted(shard, axis, by):
    peers = lax.axis_size(axis)
    pairs = [(i, i + by) for i in range(peers) if 0 <= i + by < peers]
    return lax.ppermute(shard, axis, pairs)


def entering(value, axis, join, neutral, backward):
    count, mine = (lax.axis_size(axis), lax.axis_index(axis))
    pieces = jax.tree.map(lambda part: lax.all_gather(part, axis), value)
    if backward:
        pieces = jax.tree.map(lambda part: part[::-1], pieces)
        mine = count - 1 - mine
    total = jax.tree.map(
        lambda part, zero: jnp.full_like(part, 0) + jnp.asarray(zero, part.dtype), value, neutral
    )

    def lap(position, total):
        longer = join(total, jax.tree.map(lambda part: part[position], pieces))
        return jax.tree.map(lambda new, old: jnp.where(position < mine, new, old), longer, total)

    return lax.fori_loop(0, count - 1, lap, total)


def silu(values):
    return values * jax.nn.sigmoid(values)


def silu_slope(values):
    sigmoid_value = jax.nn.sigmoid(values)
    return sigmoid_value * (1.0 + values * (1.0 - sigmoid_value))


def stretch_update(carry, pieces):
    state, decay_rate = carry
    x_block, step_block, b_block, c_block = pieces
    cumulative = jnp.cumsum(step_block * decay_rate, axis=1)
    extent = step_block.shape[1]
    row_index = lax.broadcasted_iota(jnp.int32, (extent, extent), 0)
    col_index = lax.broadcasted_iota(jnp.int32, (extent, extent), 1)
    causal = (row_index >= col_index)[None, :, :, None]
    gaps = cumulative[:, :, None, :] - cumulative[:, None, :, :]
    kernel = jnp.exp(jnp.where(causal, gaps, -1e30))
    scores = jnp.einsum("btn,bsn->bts", c_block, b_block, precision=PRECISE)
    mixing = kernel * scores[..., None] * step_block[:, None, :, :]
    inner = jnp.einsum("btsh,bshp->bthp", mixing, x_block, precision=PRECISE)
    carried = (
        jnp.einsum("btn,bhpn->bthp", c_block, state, precision=PRECISE)
        * jnp.exp(cumulative)[..., None]
    )
    tail_weight = jnp.exp(cumulative[:, -1:, :] - cumulative) * step_block
    fresh = jnp.einsum("bsh,bshp,bsn->bhpn", tail_weight, x_block, b_block, precision=PRECISE)
    state = jnp.exp(cumulative[:, -1, :])[:, :, None, None] * state + fresh
    return ((state, decay_rate), inner + carried)


def local_scan(x_part, step_sizes, b_matrix, c_matrix, decay_rate, skip_weight):
    batch_seqs, extent = (step_sizes.shape[0], step_sizes.shape[1])
    block_size = min(extent, 256)
    block_count = extent // block_size

    def split_blocks(values):
        shaped = values.reshape((batch_seqs, block_count, block_size) + values.shape[2:])
        return jnp.moveaxis(shaped, 1, 0)

    start = jnp.zeros(
        (batch_seqs, x_part.shape[2], x_part.shape[3], b_matrix.shape[2]), jnp.float32
    )
    carry_out, outputs = lax.scan(
        stretch_update,
        (start, decay_rate),
        (
            split_blocks(x_part),
            split_blocks(step_sizes),
            split_blocks(b_matrix),
            split_blocks(c_matrix),
        ),
    )
    mixed = jnp.moveaxis(outputs, 0, 1).reshape(x_part.shape) + skip_weight[:, None] * x_part
    growth = jnp.exp(jnp.cumsum(step_sizes * decay_rate, axis=1))
    return (mixed, carry_out[0], growth[:, -1, :], growth)


def join_states(earlier, later):
    return (earlier[0] * later[0], later[0][..., None, None] * earlier[1] + later[1])


def gather_rows(pair):
    return (
        lax.all_gather(pair[0], "seq", axis=0, tiled=True),
        lax.all_gather(pair[1], "seq", axis=0, tiled=True),
    )


def gram_sum(parts):
    return lax.psum((parts[0], parts[1], parts[2], parts[3]), "head")


def per_device(
    inputs,
    lengths,
    norm_gain,
    in_proj,
    conv_weight,
    conv_bias,
    head_params,
    gate_gain,
    out_proj,
    cotangent,
    norm_gain_mom,
    in_proj_mom,
    conv_weight_mom,
    conv_bias_mom,
    head_params_mom,
    gate_gain_mom,
    out_proj_mom,
):
    batch_seqs, extent, model_width = inputs.shape
    seq_count = lax.axis_size("seq")
    head_count = lax.axis_size("head")
    seq_place = lax.axis_index("seq")
    heads_here = head_params.shape[1]
    head_span = gate_gain.shape[0]
    head_size = head_span // heads_here
    channels = conv_bias.shape[0]
    state_size = (channels - head_span) * head_count // 2
    inner_all = head_span * head_count
    group_cols = in_proj.shape[1]
    proj_all = group_cols * head_count
    tap_count = conv_weight.shape[0]
    share = model_width // seq_count
    positions = seq_place * extent + lax.broadcasted_iota(jnp.int32, (batch_seqs, extent), 1)
    valid_mask = (positions < lengths[:, None]).astype(jnp.float32)[..., None]
    data = inputs.astype(jnp.float32)
    root_scale = lax.rsqrt(jnp.mean(data * data, axis=-1, keepdims=True) + EPSILON)
    normed = data * root_scale
    lowered = (normed * norm_gain).astype(jnp.bfloat16)
    in_low = in_proj.astype(jnp.bfloat16)
    projected = jnp.einsum("bld,dk->blk", lowered, in_low, preferred_element_type=jnp.float32)
    z_part = projected[..., :head_span]
    conv_in = projected[..., head_span : head_span + channels].astype(jnp.bfloat16)
    raw_steps = projected[..., head_span + channels :]
    before = shifted(conv_in[:, extent - tap_count + 1 :], "seq", 1)
    padded = jnp.concatenate([before, conv_in], axis=1)
    conv_out = conv_bias + jnp.zeros(conv_in.shape, jnp.float32)
    for offset in range(tap_count):
        conv_out = conv_out + conv_weight[offset] * padded[:, offset : offset + extent]
    activated = silu(conv_out)
    x_heads = activated[..., :head_span].reshape(batch_seqs, extent, heads_here, head_size)
    bc_local = activated[..., head_span:].astype(jnp.bfloat16)
    bc_full = lax.all_gather(bc_local, "head", axis=2, tiled=True).astype(jnp.float32)
    b_matrix = bc_full[..., :state_size]
    c_matrix = bc_full[..., state_size:]
    pre_steps = raw_steps + head_params[0]
    step_sizes = jax.nn.softplus(pre_steps)
    decay_rate = -jnp.exp(head_params[1])
    (mixed_local, state_local, block_decay, growth), pullback = jax.vjp(
        local_scan, x_heads, step_sizes, b_matrix, c_matrix, decay_rate, head_params[2]
    )
    identity = (jnp.ones_like(block_decay), jnp.zeros_like(state_local))
    decay_in, state_in = entering((block_decay, state_local), "seq", join_states, identity, False)
    from_state = jnp.einsum("bln,bhpn->blhp", c_matrix, state_in, precision=PRECISE)
    mixed = mixed_local + from_state * growth[..., None]
    mixed_flat = mixed.reshape(batch_seqs, extent, head_span)
    gate_value = silu(z_part)
    gated = mixed_flat * gate_value
    squares = jnp.sum(gated * gated, axis=-1)
    gated_low = (gated * gate_gain).astype(jnp.bfloat16)
    out_low = out_proj.astype(jnp.bfloat16)
    partial_out = jnp.einsum("blk,kd->bld", gated_low, out_low, preferred_element_type=jnp.float32)
    summed, square_sum = lax.psum((partial_out, squares), "head")
    norm_scale = lax.rsqrt(square_sum / inner_all + EPSILON)[..., None]
    result = valid_mask * (data + norm_scale * summed)
    output = result.astype(jnp.bfloat16)
    result_squares = jnp.sum(result * result)
    back_grad = cotangent.astype(jnp.float32) * valid_mask
    grad_summed = (norm_scale * back_grad).astype(jnp.bfloat16)
    grad_scale = jnp.sum(back_grad * summed, axis=-1, keepdims=True)
    grad_low = jnp.einsum("bld,kd->blk", grad_summed, out_low, preferred_element_type=jnp.float32)
    grad_gated = (
        grad_low * gate_gain - grad_scale * norm_scale * norm_scale * norm_scale * gated / inner_all
    )
    gate_gain_grad = jnp.sum(grad_low * gated, axis=(0, 1))
    grad_mixed = (grad_gated * gate_value).reshape(batch_seqs, extent, heads_here, head_size)
    grad_z = grad_gated * mixed_flat * silu_slope(z_part)
    grad_growth = jnp.sum(grad_mixed * from_state, axis=-1)
    weighted = grad_mixed * growth[..., None]
    grad_c_extra = jnp.einsum("blhp,bhpn->bln", weighted, state_in, precision=PRECISE)
    grad_state_here = jnp.einsum("blhp,bln->bhpn", weighted, c_matrix, precision=PRECISE)
    decay_out, grad_state_end = entering(
        (block_decay, grad_state_here), "seq", join_states, identity, True
    )
    grad_decay = jnp.sum(grad_state_end * state_in, axis=(2, 3))
    grad_x, grad_steps, grad_b, grad_c, grad_rate, grad_skip = pullback(
        (grad_mixed, grad_state_end, grad_decay, grad_growth)
    )
    grad_bc = jnp.concatenate([grad_b, grad_c + grad_c_extra], axis=-1)
    grad_bc_local = lax.psum_scatter(grad_bc, "head", scatter_dimension=2, tiled=True)
    grad_pre = grad_steps * jax.nn.sigmoid(pre_steps)
    head_params_grad = jnp.stack(
        [jnp.sum(grad_pre, axis=(0, 1)), grad_rate * decay_rate, grad_skip]
    )
    grad_activated = jnp.concatenate(
        [grad_x.reshape(batch_seqs, extent, head_span), grad_bc_local], axis=-1
    )
    grad_conv = (grad_activated * silu_slope(conv_out)).astype(jnp.bfloat16)
    after = shifted(grad_conv[:, : tap_count - 1], "seq", -1)
    trailing = jnp.concatenate([grad_conv, after], axis=1)
    grad_conv_wide = grad_conv.astype(jnp.float32)
    grad_conv_in = jnp.zeros(conv_in.shape, jnp.float32)
    tap_grads = []
    for offset in range(tap_count):
        lead = tap_count - 1 - offset
        grad_conv_in = grad_conv_in + conv_weight[offset] * trailing[:, lead : lead + extent]
        tap_grads.append(jnp.sum(grad_conv_wide * padded[:, offset : offset + extent], axis=(0, 1)))
    conv_weight_grad = jnp.stack(tap_grads)
    conv_bias_grad = jnp.sum(grad_conv_wide, axis=(0, 1))
    grad_projected = jnp.concatenate([grad_z, grad_conv_in, grad_pre], axis=-1).astype(jnp.bfloat16)
    partial_in = jnp.einsum(
        "blk,dk->bld", grad_projected, in_low, preferred_element_type=jnp.float32
    )
    grad_lowered = lax.psum(partial_in, "head")
    norm_gain_grad = jnp.sum(grad_lowered * normed, axis=(0, 1))
    grad_normed = grad_lowered * norm_gain
    input_grad = back_grad + root_scale * (
        grad_normed - normed * jnp.mean(grad_normed * normed, axis=-1, keepdims=True)
    )
    token_rows = batch_seqs * extent
    lowered_rows = lowered.reshape(token_rows, model_width)
    grad_proj_rows = grad_projected.reshape(token_rows, group_cols)
    grad_sum_rows = grad_summed.reshape(token_rows, model_width)
    gated_rows = gated_low.reshape(token_rows, head_span)
    whole_term = jnp.concatenate(
        [
            jnp.einsum(
                "td,tk->dk", lowered_rows, grad_proj_rows, preferred_element_type=jnp.float32
            ),
            jnp.einsum("td,tk->dk", grad_sum_rows, gated_rows, preferred_element_type=jnp.float32),
        ],
        axis=1,
    )
    whole_sum = lax.psum(whole_term, "seq")
    rows_here = lax.dynamic_slice_in_dim(whole_sum, seq_place * share, share, 0)
    in_proj_grad = rows_here[:, :group_cols]
    out_grad_rows = rows_here[:, group_cols:]
    small_sums = lax.psum(
        (
            norm_gain_grad,
            conv_weight_grad,
            conv_bias_grad,
            head_params_grad,
            gate_gain_grad,
            result_squares,
        ),
        "seq",
    )
    (
        norm_gain_grad,
        conv_weight_grad,
        conv_bias_grad,
        head_params_grad,
        gate_gain_grad,
        squares_all,
    ) = small_sums
    rms = jnp.sqrt(squares_all / (jnp.sum(lengths).astype(jnp.float32) * model_width))
    in_proj_mom_new = 0.5 * in_proj_mom + in_proj_grad
    out_rows_mom = 0.5 * out_proj_mom.T + out_grad_rows
    rows_in, rows_out = (in_proj_mom_new, out_rows_mom)
    full_in, full_out = gather_rows((rows_in, rows_out))
    for iteration in range(NS_STEPS):
        gram_in = jnp.dot(rows_in, full_in.T, precision=PRECISE)
        gram_out = jnp.dot(rows_out, full_out.T, precision=PRECISE)
        gram_in, gram_out, size_in, size_out = gram_sum(
            (gram_in, gram_out, jnp.sum(full_in * full_in), jnp.sum(full_out * full_out))
        )
        if iteration == 0:
            factor_in = 1.0 / (jnp.sqrt(size_in) + 1e-07)
            factor_out = 1.0 / (jnp.sqrt(size_out) + 1e-07)
            rows_in = rows_in * factor_in
            full_in = full_in * factor_in
            gram_in = gram_in * factor_in * factor_in
            rows_out = rows_out * factor_out
            full_out = full_out * factor_out
            gram_out = gram_out * factor_out * factor_out
        image_in = jnp.dot(gram_in, full_in, precision=PRECISE)
        image_out = jnp.dot(gram_out, full_out, precision=PRECISE)
        image_full_in, image_full_out = gather_rows((image_in, image_out))
        rows_in = (
            COEF_A * rows_in
            + COEF_B * image_in
            + COEF_C * jnp.dot(gram_in, image_full_in, precision=PRECISE)
        )
        rows_out = (
            COEF_A * rows_out
            + COEF_B * image_out
            + COEF_C * jnp.dot(gram_out, image_full_out, precision=PRECISE)
        )
        if iteration + 1 < NS_STEPS:
            full_in, full_out = gather_rows((rows_in, rows_out))
    in_old_rows = lax.dynamic_slice_in_dim(in_proj, seq_place * share, share, 0)
    in_proj_new = in_old_rows - MUON_RATE * 0.2 * math.sqrt(max(model_width, proj_all)) * rows_in
    out_old_cols = lax.dynamic_slice_in_dim(out_proj, seq_place * share, share, 1)
    out_proj_new = (
        out_old_cols - MUON_RATE * 0.2 * math.sqrt(max(inner_all, model_width)) * rows_out.T
    )
    divisor = math.sqrt(batch_seqs * extent * seq_count)
    norm_gain_mom_new = 0.5 * norm_gain_mom + norm_gain_grad
    conv_weight_mom_new = 0.5 * conv_weight_mom + conv_weight_grad
    conv_bias_mom_new = 0.5 * conv_bias_mom + conv_bias_grad
    head_params_mom_new = 0.5 * head_params_mom + head_params_grad
    gate_gain_mom_new = 0.5 * gate_gain_mom + gate_gain_grad
    norm_gain_new = norm_gain - SMALL_RATE * norm_gain_mom_new / divisor
    conv_weight_new = conv_weight - SMALL_RATE * conv_weight_mom_new / divisor
    conv_bias_new = conv_bias - SMALL_RATE * conv_bias_mom_new / divisor
    head_params_new = head_params - SMALL_RATE * head_params_mom_new / divisor
    gate_gain_new = gate_gain - SMALL_RATE * gate_gain_mom_new / divisor
    return (
        output,
        input_grad,
        norm_gain_grad,
        in_proj_grad,
        conv_weight_grad,
        conv_bias_grad,
        head_params_grad,
        gate_gain_grad,
        out_grad_rows.T,
        norm_gain_mom_new,
        in_proj_mom_new,
        conv_weight_mom_new,
        conv_bias_mom_new,
        head_params_mom_new,
        gate_gain_mom_new,
        out_rows_mom.T,
        norm_gain_new,
        in_proj_new,
        conv_weight_new,
        conv_bias_new,
        head_params_new,
        gate_gain_new,
        out_proj_new,
        rms,
    )


def solution(mesh):
    return jax.shard_map(
        per_device,
        mesh=mesh,
        in_specs=(
            P(None, "seq", None),
            P(),
            P(),
            P(None, "head"),
            P(None, "head"),
            P("head"),
            P(None, "head"),
            P("head"),
            P("head", None),
            P(None, "seq", None),
            P(),
            P("seq", "head"),
            P(None, "head"),
            P("head"),
            P(None, "head"),
            P("head"),
            P("head", "seq"),
        ),
        out_specs=(
            P(None, "seq", None),
            P(None, "seq", None),
            P(),
            P("seq", "head"),
            P(None, "head"),
            P("head"),
            P(None, "head"),
            P("head"),
            P("head", "seq"),
            P(),
            P("seq", "head"),
            P(None, "head"),
            P("head"),
            P(None, "head"),
            P("head"),
            P("head", "seq"),
            P(),
            P("seq", "head"),
            P(None, "head"),
            P("head"),
            P(None, "head"),
            P("head"),
            P("head", "seq"),
            P(),
        ),
        check_vma=False,
    )
```

profile of v0, /device:TPU:0, one launch (start us, length us, event | category | flops | bytes accessed | tf_op | source)
XLA Modules:
  0.0 2182.6 jit_solution(4297151667985426974)
XLA Ops:
  56.4 31.3 %all-gather = f32[64,1,6]{2,1,0:T(1,128)S(1)} all-gather(f32[8,1,6]{2,1,0:T(1,128)S(1)} %copy.321), channel_id=2, replica_groups=mesh['seq'=8,'head'=4] {'seq'}, dimensions={0}, use_global_device_ids=true | all-gather | bytes 1728 | tf_op jit(solution)/shard_map/all_gather | solution.py:28
  93.9 138.9 %all-gather.69.cloned.1.call-done = f32[64,6,64,128]{3,2,1,0:T(8,128)} async-done(((f32[8,6,64,128]{3,2,1,0:T(8,128)}), f32[64,6,64,128]{3,2,1,0:T(8,128)}) %all-gather.69.cloned.1.call-update) | async-done | bytes 12582928 | tf_op jit(solution)/shard_map/all_gather | solution.py:28
  282.1 110.5 %all-reduce.18.cloned.1.call-done = f32[8,256,768]{2,1,0:T(8,128)} async-done(((f32[8,256,768]{2,1,0:T(8,128)}), f32[8,256,768]{2,1,0:T(8,128)}) %all-reduce.18.cloned.1.call-update) | async-done | bytes 6291472 | tf_op jit(solution)/shard_map/psum | solution.py:189
  423.0 20.5 fusion.14
  447.1 143.5 %all-gather.71.cloned.1.call-done = f32[64,6,64,128]{3,2,1,0:T(8,128)} async-done(((f32[8,6,64,128]{3,2,1,0:T(8,128)}), f32[64,6,64,128]{3,2,1,0:T(8,128)}) %all-gather.71.cloned.1.call-update) | async-done | bytes 12582928 | tf_op jit(solution)/shard_map/all_gather | solution.py:28
  602.5 18.4 while.19
  725.2 148.7 %all-reduce.20.cloned.1.call-done = f32[768,1222]{1,0:T(8,128)} async-done(((f32[768,1222]{1,0:T(8,128)}), f32[768,1222]{1,0:T(8,128)}) %all-reduce.20.cloned.1.call-update) | async-done | bytes 3754000 | tf_op jit(solution)/shard_map/psum | solution.py:260
  877.8 39.2 %all-gather.49.cloned.1.call-done = f32[768,384]{1,0:T(8,128)} async-done(((f32[96,384]{1,0:T(8,128)}), f32[768,384]{1,0:T(8,128)}) %all-gather.49.cloned.1.call-update) | async-done | bytes 1179664 | tf_op jit(solution)/shard_map/all_gather | solution.py:109
  920.3 54.5 %all-gather.29.cloned.1.call-done = f32[768,838]{1,0:T(8,128)} async-done(((f32[96,838]{1,0:T(8,128)}), f32[768,838]{1,0:T(8,128)}) %all-gather.29.cloned.1.call-update) | async-done | bytes 2574352 | tf_op jit(solution)/shard_map/all_gather | solution.py:108
  992.5 20.2 all-reduce.30.cloned.1.call-done
  1021.1 35.8 %all-gather.51.cloned.1.call-done = f32[768,384]{1,0:T(8,128)} async-done(((f32[96,384]{1,0:T(8,128)}), f32[768,384]{1,0:T(8,128)}) %all-gather.51.cloned.1.call-update) | async-done | bytes 1179664 | tf_op jit(solution)/shard_map/all_gather | solution.py:109
  1059.9 54.9 %all-gather.31.cloned.1.call-done = f32[768,838]{1,0:T(8,128)} async-done(((f32[96,838]{1,0:T(8,128)}), f32[768,838]{1,0:T(8,128)}) %all-gather.31.cloned.1.call-update) | async-done | bytes 2574352 | tf_op jit(solution)/shard_map/all_gather | solution.py:108
  1119.0 38.2 %all-gather.53.cloned.1.call-done = f32[768,384]{1,0:T(8,128)} async-done(((f32[96,384]{1,0:T(8,128)}), f32[768,384]{1,0:T(8,128)}) %all-gather.53.cloned.1.call-update) | async-done | bytes 1179664 | tf_op jit(solution)/shard_map/all_gather | solution.py:109
  1160.6 54.5 %all-gather.33.cloned.1.call-done = f32[768,838]{1,0:T(8,128)} async-done(((f32[96,838]{1,0:T(8,128)}), f32[768,838]{1,0:T(8,128)}) %all-gather.33.cloned.1.call-update) | async-done | bytes 2574352 | tf_op jit(solution)/shard_map/all_gather | solution.py:108
  1220.5 32.4 %all-reduce.28.cloned.1.call-done = (f32[96,768]{1,0:T(8,128)}, f32[96,768]{1,0:T(8,128)}) async-done(((f32[96,768]{1,0:T(8,128)}, f32[96,768]{1,0:T(8,128)}), (f32[96,768]{1,0:T(8,128)}, f32[96,768]{1,0:T(8,128)})) %all-reduce.28.cloned.1.call-update) | async-done | bytes 589840 | tf_op jit(solution)/shard_map/psum | solution.py:114
  1260.1 36.8 %all-gather.55.cloned.1.call-done = f32[768,384]{1,0:T(8,128)} async-done(((f32[96,384]{1,0:T(8,128)}), f32[768,384]{1,0:T(8,128)}) %all-gather.55.cloned.1.call-update) | async-done | bytes 1179664 | tf_op jit(solution)/shard_map/all_gather | solution.py:109
  1300.3 54.3 %all-gather.35.cloned.1.call-done = f32[768,838]{1,0:T(8,128)} async-done(((f32[96,838]{1,0:T(8,128)}), f32[768,838]{1,0:T(8,128)}) %all-gather.35.cloned.1.call-update) | async-done | bytes 2574352 | tf_op jit(solution)/shard_map/all_gather | solution.py:108
  1359.0 38.2 %all-gather.57.cloned.1.call-done = f32[768,384]{1,0:T(8,128)} async-done(((f32[96,384]{1,0:T(8,128)}), f32[768,384]{1,0:T(8,128)}) %all-gather.57.cloned.1.call-update) | async-done | bytes 1179664 | tf_op jit(solution)/shard_map/all_gather | solution.py:109
  1400.5 54.4 %all-gather.37.cloned.1.call-done = f32[768,838]{1,0:T(8,128)} async-done(((f32[96,838]{1,0:T(8,128)}), f32[768,838]{1,0:T(8,128)}) %all-gather.37.cloned.1.call-update) | async-done | bytes 2574352 | tf_op jit(solution)/shard_map/all_gather | solution.py:108
  1460.3 32.3 %all-reduce.26.cloned.1.call-done = (f32[96,768]{1,0:T(8,128)}, f32[96,768]{1,0:T(8,128)}) async-done(((f32[96,768]{1,0:T(8,128)}, f32[96,768]{1,0:T(8,128)}), (f32[96,768]{1,0:T(8,128)}, f32[96,768]{1,0:T(8,128)})) %all-reduce.26.cloned.1.call-update) | async-done | bytes 589840 | tf_op jit(solution)/shard_map/psum | solution.py:114
  1499.8 36.8 %all-gather.59.cloned.1.call-done = f32[768,384]{1,0:T(8,128)} async-done(((f32[96,384]{1,0:T(8,128)}), f32[768,384]{1,0:T(8,128)}) %all-gather.59.cloned.1.call-update) | async-done | bytes 1179664 | tf_op jit(solution)/shard_map/all_gather | solution.py:109
  1539.6 54.9 %all-gather.39.cloned.1.call-done = f32[768,838]{1,0:T(8,128)} async-done(((f32[96,838]{1,0:T(8,128)}), f32[768,838]{1,0:T(8,128)}) %all-gather.39.cloned.1.call-update) | async-done | bytes 2574352 | tf_op jit(solution)/shard_map/all_gather | solution.py:108
  1599.0 38.2 %all-gather.61.cloned.1.call-done = f32[768,384]{1,0:T(8,128)} async-done(((f32[96,384]{1,0:T(8,128)}), f32[768,384]{1,0:T(8,128)}) %all-gather.61.cloned.1.call-update) | async-done | bytes 1179664 | tf_op jit(solution)/shard_map/all_gather | solution.py:109
  1640.5 54.5 %all-gather.41.cloned.1.call-done = f32[768,838]{1,0:T(8,128)} async-done(((f32[96,838]{1,0:T(8,128)}), f32[768,838]{1,0:T(8,128)}) %all-gather.41.cloned.1.call-update) | async-done | bytes 2574352 | tf_op jit(solution)/shard_map/all_gather | solution.py:108
  1700.4 32.3 %all-reduce.24.cloned.1.call-done = (f32[96,768]{1,0:T(8,128)}, f32[96,768]{1,0:T(8,128)}) async-done(((f32[96,768]{1,0:T(8,128)}, f32[96,768]{1,0:T(8,128)}), (f32[96,768]{1,0:T(8,128)}, f32[96,768]{1,0:T(8,128)})) %all-reduce.24.cloned.1.call-update) | async-done | bytes 589840 | tf_op jit(solution)/shard_map/psum | solution.py:114
  1740.0 36.8 %all-gather.63.cloned.1.call-done = f32[768,384]{1,0:T(8,128)} async-done(((f32[96,384]{1,0:T(8,128)}), f32[768,384]{1,0:T(8,128)}) %all-gather.63.cloned.1.call-update) | async-done | bytes 1179664 | tf_op jit(solution)/shard_map/all_gather | solution.py:109
  1779.8 54.7 %all-gather.43.cloned.1.call-done = f32[768,838]{1,0:T(8,128)} async-done(((f32[96,838]{1,0:T(8,128)}), f32[768,838]{1,0:T(8,128)}) %all-gather.43.cloned.1.call-update) | async-done | bytes 2574352 | tf_op jit(solution)/shard_map/all_gather | solution.py:108
  1848.1 28.9 %all-gather.65.cloned.1.call-done = f32[768,384]{1,0:T(8,128)} async-done(((f32[96,384]{1,0:T(8,128)}), f32[768,384]{1,0:T(8,128)}) %all-gather.65.cloned.1.call-update) | async-done | bytes 1179664 | tf_op jit(solution)/shard_map/all_gather | solution.py:109
  1880.3 54.5 %all-gather.45.cloned.1.call-done = f32[768,838]{1,0:T(8,128)} async-done(((f32[96,838]{1,0:T(8,128)}), f32[768,838]{1,0:T(8,128)}) %all-gather.45.cloned.1.call-update) | async-done | bytes 2574352 | tf_op jit(solution)/shard_map/all_gather | solution.py:108
  1940.1 128.2 %all-reduce.22.cloned.1.call-done = (f32[8,256,768]{2,1,0:T(8,128)}, f32[96,768]{1,0:T(8,128)}, f32[96,768]{1,0:T(8,128)}) async-done(((f32[8,256,768]{2,1,0:T(8,128)}, f32[96,768]{1,0:T(8,128)}, f32[96,768]{1,0:T(8,128)}), (f32[8,256,768]{2,1,0:T(8,128)}, f32[96,768]{1,0:T(8,128)}, f32[96,768]{1,0:T(8,128)})) %all-reduce.22.cloned.1.call-update) | async-done | bytes 6881296 | tf_op jit(solution)/shard_map/psum | solution.py:240
  2089.3 38.7 %all-reduce.3 = (f32[768]{0:T(1024)}, f32[4,448]{1,0:T(4,128)}, f32[448]{0:T(512)}, f32[3,6]{1,0:T(4,128)}, f32[384]{0:T(512)}, /*index=5*/f32[]{:T(128)}) all-reduce(f32[768]{0:T(1024)S(1)} %get-tuple-element.546, f32[4,448]{1,0:T(4,128)S(1)} %pad_maximum_fusion.7, ...), channel_id=1, replica_groups=mesh['seq'=8,'head'=4] {'seq'}, use_global_device_ids=true, to_apply=%region_28.29 | all-reduce | flops 3411 | bytes 27288 | tf_op jit(solution)/shard_map/psum | solution.py:264
  2144.9 25.2 %all-gather.47.cloned.1.call-done = f32[768,838]{1,0:T(8,128)} async-done(((f32[96,838]{1,0:T(8,128)}), f32[768,838]{1,0:T(8,128)}) %all-gather.47.cloned.1.call-update) | async-done | bytes 2574352 | tf_op jit(solution)/shard_map/all_gather | solution.py:108
  (407 shorter events, 451.8 us)
Async XLA Ops:
  7.2 45.0 %all-gather.27.cloned.1.call-start = ((), (), s32[]{:S(2)}) async-start(), calls=%async_computation.1 | async-start | bytes 1310720 | tf_op jit(solution)/shard_map/all_gather | solution.py:169
  19.2 6.6 collective-permute-start
  33.5 199.3 %all-gather.69.cloned.1.call-start = ((), (), s32[]{:S(2)}) async-start(), calls=%async_computation.25 | async-start | bytes 14155776 | tf_op jit(solution)/shard_map/all_gather | solution.py:28
  56.1 336.5 %all-reduce.18.cloned.1.call-start = ((), (), s32[]{:S(2)}) async-start(), calls=%async_computation.2 | async-start | bytes 12582912 | tf_op jit(solution)/shard_map/psum | solution.py:189
  274.7 315.9 %all-gather.71.cloned.1.call-start = ((), (), s32[]{:S(2)}) async-start(), calls=%async_computation.26 | async-start | bytes 14155776 | tf_op jit(solution)/shard_map/all_gather | solution.py:28
  413.8 276.2 %reduce-scatter.2.cloned.1.call-start = ((), (), s32[]{:S(2)}) async-start(), calls=%async_computation.3 | async-start | bytes 2621440 | tf_op jit(solution)/shard_map/reduce_scatter | solution.py:216
  628.8 245.1 %all-reduce.20.cloned.1.call-start = ((), (), s32[]{:S(2)}) async-start(), calls=%async_computation.4 | async-start | bytes 7864320 | tf_op jit(solution)/shard_map/psum | solution.py:260
  725.1 191.9 %all-gather.49.cloned.1.call-start = ((), (), s32[]{:S(2)}) async-start(), calls=%async_computation.15 | async-start | bytes 1327104 | tf_op jit(solution)/shard_map/all_gather | solution.py:109
  875.8 99.1 %all-gather.29.cloned.1.call-start = ((), (), s32[]{:S(2)}) async-start(), calls=%async_computation.5 | async-start | bytes 3096576 | tf_op jit(solution)/shard_map/all_gather | solution.py:108
  877.7 135.0 %all-reduce.30.cloned.1.call-start = ((), (), s32[]{:S(2)}) async-start(), calls=%async_computation.31 | async-start | bytes 1179648 | tf_op jit(solution)/shard_map/psum | solution.py:114
  980.2 76.7 %all-gather.51.cloned.1.call-start = ((), (), s32[]{:S(2)}) async-start(), calls=%async_computation.16 | async-start | bytes 1327104 | tf_op jit(solution)/shard_map/all_gather | solution.py:109
  1015.7 99.0 %all-gather.31.cloned.1.call-start = ((), (), s32[]{:S(2)}) async-start(), calls=%async_computation.6 | async-start | bytes 3096576 | tf_op jit(solution)/shard_map/all_gather | solution.py:108
  1021.0 136.3 %all-gather.53.cloned.1.call-start = ((), (), s32[]{:S(2)}) async-start(), calls=%async_computation.17 | async-start | bytes 1327104 | tf_op jit(solution)/shard_map/all_gather | solution.py:109
  1059.8 155.3 %all-gather.33.cloned.1.call-start = ((), (), s32[]{:S(2)}) async-start(), calls=%async_computation.7 | async-start | bytes 3096576 | tf_op jit(solution)/shard_map/all_gather | solution.py:108
  1119.0 133.9 %all-reduce.28.cloned.1.call-start = ((), (), s32[]{:S(2)}) async-start(), calls=%async_computation.30 | async-start | bytes 1179648 | tf_op jit(solution)/shard_map/psum | solution.py:114
  1220.5 76.5 %all-gather.55.cloned.1.call-start = ((), (), s32[]{:S(2)}) async-start(), calls=%async_computation.18 | async-start | bytes 1327104 | tf_op jit(solution)/shard_map/all_gather | solution.py:109
  1255.7 98.9 %all-gather.35.cloned.1.call-start = ((), (), s32[]{:S(2)}) async-start(), calls=%async_computation.8 | async-start | bytes 3096576 | tf_op jit(solution)/shard_map/all_gather | solution.py:108
  1260.1 137.1 %all-gather.57.cloned.1.call-start = ((), (), s32[]{:S(2)}) async-start(), calls=%async_computation.19 | async-start | bytes 1327104 | tf_op jit(solution)/shard_map/all_gather | solution.py:109
  1299.9 155.0 %all-gather.37.cloned.1.call-start = ((), (), s32[]{:S(2)}) async-start(), calls=%async_computation.9 | async-start | bytes 3096576 | tf_op jit(solution)/shard_map/all_gather | solution.py:108
  1358.9 133.7 %all-reduce.26.cloned.1.call-start = ((), (), s32[]{:S(2)}) async-start(), calls=%async_computation.29 | async-start | bytes 1179648 | tf_op jit(solution)/shard_map/psum | solution.py:114
  1460.2 76.4 %all-gather.59.cloned.1.call-start = ((), (), s32[]{:S(2)}) async-start(), calls=%async_computation.20 | async-start | bytes 1327104 | tf_op jit(solution)/shard_map/all_gather | solution.py:109
  1495.4 99.0 %all-gather.39.cloned.1.call-start = ((), (), s32[]{:S(2)}) async-start(), calls=%async_computation.10 | async-start | bytes 3096576 | tf_op jit(solution)/shard_map/all_gather | solution.py:108
  1499.8 137.4 %all-gather.61.cloned.1.call-start = ((), (), s32[]{:S(2)}) async-start(), calls=%async_computation.21 | async-start | bytes 1327104 | tf_op jit(solution)/shard_map/all_gather | solution.py:109
  1539.6 155.5 %all-gather.41.cloned.1.call-start = ((), (), s32[]{:S(2)}) async-start(), calls=%async_computation.11 | async-start | bytes 3096576 | tf_op jit(solution)/shard_map/all_gather | solution.py:108
  1598.7 134.0 %all-reduce.24.cloned.1.call-start = ((), (), s32[]{:S(2)}) async-start(), calls=%async_computation.28 | async-start | bytes 1179648 | tf_op jit(solution)/shard_map/psum | solution.py:114
  1700.4 76.4 %all-gather.63.cloned.1.call-start = ((), (), s32[]{:S(2)}) async-start(), calls=%async_computation.22 | async-start | bytes 1327104 | tf_op jit(solution)/shard_map/all_gather | solution.py:109
  1735.6 98.9 %all-gather.43.cloned.1.call-start = ((), (), s32[]{:S(2)}) async-start(), calls=%async_computation.12 | async-start | bytes 3096576 | tf_op jit(solution)/shard_map/all_gather | solution.py:108
  1739.9 137.1 %all-gather.65.cloned.1.call-start = ((), (), s32[]{:S(2)}) async-start(), calls=%async_computation.23 | async-start | bytes 1327104 | tf_op jit(solution)/shard_map/all_gather | solution.py:109
  1779.7 155.1 %all-gather.45.cloned.1.call-start = ((), (), s32[]{:S(2)}) async-start(), calls=%async_computation.13 | async-start | bytes 3096576 | tf_op jit(solution)/shard_map/all_gather | solution.py:108
  1838.8 229.6 %all-reduce.22.cloned.1.call-start = ((), (), s32[]{:S(2)}) async-start(), calls=%async_computation.27 | async-start | bytes 13762560 | tf_op jit(solution)/shard_map/psum | solution.py:240
  1940.1 201.6 %all-gather.67.cloned.1.call-start = ((), (), s32[]{:S(2)}) async-start(), calls=%async_computation.24 | async-start | bytes 1327104 | tf_op jit(solution)/shard_map/all_gather | solution.py:109
  2071.3 98.7 %all-gather.47.cloned.1.call-start = ((), (), s32[]{:S(2)}) async-start(), calls=%async_computation.14 | async-start | bytes 3096576 | tf_op jit(solution)/shard_map/all_gather | solution.py:108
  (79 other events, 1983.2 us)
Sparse Core Ops, SparseCore 0:
  33.6 18.5 all-gather.26
  56.2 176.5 all-gather.68
  274.8 117.7 all-reduce.17
  413.9 176.6 all-gather.70
  628.9 29.6 reduce-scatter.1
  725.3 148.6 all-reduce.19
  876.9 40.0 all-gather.48
  920.0 54.7 all-gather.28
  980.3 32.3 all-reduce.29
  1015.8 41.0 all-gather.50
  1059.9 54.7 all-gather.30
  1117.6 39.6 all-gather.52
  1160.3 54.7 all-gather.32
  1220.6 32.2 all-reduce.27
  1255.9 41.0 all-gather.54
  1299.8 54.7 all-gather.34
  1357.5 39.6 all-gather.56
  1400.0 54.7 all-gather.36
  1460.3 32.1 all-reduce.25
  1495.6 41.0 all-gather.58
  1539.6 54.7 all-gather.38
  1597.5 39.6 all-gather.60
  1640.2 54.7 all-gather.40
  1700.5 32.1 all-reduce.23
  1735.7 41.0 all-gather.62
  1779.6 54.7 all-gather.42
  1837.3 39.6 all-gather.64
  1880.0 54.7 all-gather.44
  1940.2 128.1 all-reduce.21
  2071.4 41.5 all-gather.66
  2115.2 54.8 all-gather.46
where the time goes:
time: 2190 us; the launch traced here: 2180 us
  waiting for transfers between devices  1650 us (75%)
  matrix products  238 us (11%)
  other arithmetic  135 us (6%)
  blocking collectives  83 us (4%)
  local copies, waits for them, and re-layouts  50.5 us (2%)
    all_gather x10, waiting for transfers between devices, gather_rows(): lax.all_gather(pair[0], 'seq', axis=0, tiled=True)  516 us
    all_gather x10, waiting for transfers between devices, gather_rows(): lax.all_gather(pair[1], 'seq', axis=0, tiled=True)  329 us
    all_gather x2, waiting for transfers between devices, entering(): pieces = jax.tree.map(lambda part: lax.all_gather(part, axis), value)  282 us
    psum x1, waiting for transfers between devices, per_device(): whole_sum = lax.psum(whole_term, 'seq')  149 us
    psum x1, waiting for transfers between devices, per_device(): grad_lowered = lax.psum(partial_in, 'head')  128 us
    psum x4, waiting for transfers between devices, gram_sum(): return lax.psum((parts[0], parts[1], parts[2], parts[3]), 'head')  117 us
    psum x1, waiting for transfers between devices, per_device(): summed, square_sum = lax.psum((partial_out, squares), 'head')  110 us
    dot_general x3, matrix products, stretch_update(): inner = jnp.einsum('btsh,bshp->bthp', mixing, x_block, precision=PRECISE)  50 us
  transfers between devices with their start and end apart: 33, of which 30 were waited for; matrix products, arithmetic and copies ran while one was open for 10% of the time, Pallas kernels for 0%

commit v1 on v0

v1 whole, which is shorter than its diff:
```python
import math

import jax
import jax.numpy as jnp
from jax import lax
from jax.sharding import PartitionSpec as P

NS_STEPS = 5
EPSILON = 1e-05
COEF_A = 3.4445
COEF_B = -4.775
COEF_C = 2.0315
MUON_RATE = 0.2
SMALL_RATE = 0.2
PRECISE = lax.Precision.HIGHEST
BF = jnp.bfloat16
F32 = jnp.float32


def silu(values):
    return values * jax.nn.sigmoid(values)


def silu_slope(values):
    sigmoid_value = jax.nn.sigmoid(values)
    return sigmoid_value * (1.0 + values * (1.0 - sigmoid_value))


def flip(value, axis, bit):
    count = lax.axis_size(axis)
    return lax.ppermute(value, axis, [(i, i ^ bit) for i in range(count)])


def sum_over(value, axis):
    bit = 1
    while bit < lax.axis_size(axis):
        value = jax.tree.map(lambda part: part + flip(part, axis, bit), value)
        bit *= 2
    return value


def pick(stacked, index, axis):
    return lax.dynamic_index_in_dim(stacked, index, axis, keepdims=False)


def gather_head(piece, axis):
    place = lax.axis_index("head")
    across = flip(piece, "head", 2)
    beside = flip(piece, "head", 1)
    corner = flip(across, "head", 1)
    low, high = place % 2, place // 2
    near = jnp.where(low == 0, jnp.stack([piece, beside], axis), jnp.stack([beside, piece], axis))
    far = jnp.where(low == 0, jnp.stack([across, corner], axis), jnp.stack([corner, across], axis))
    return jnp.where(
        high == 0, jnp.concatenate([near, far], axis), jnp.concatenate([far, near], axis)
    )


def scatter_head(parts, axis, wire):
    place = lax.axis_index("head")
    low, high = place % 2, place // 2
    shape = parts.shape
    parts = parts.reshape(shape[:axis] + (2, 2) + shape[axis + 1 :])
    half = pick(parts, low, axis + 1) + flip(pick(parts, 1 - low, axis + 1), "head", 1)
    sent = flip(pick(half, 1 - high, axis).astype(wire), "head", 2)
    return pick(half, high, axis) + sent.astype(F32)


def spread(blocks, members):
    count = lax.axis_size("seq")
    runs = [list(range(i, i + members)) for i in range(0, count, members)]
    return lax.all_to_all(
        blocks, "seq", 0, 0, tiled=True, axis_index_groups=runs if len(runs) > 1 else None
    )


def stretch_update(carry, pieces):
    state, decay_rate = carry
    x_block, step_block, b_block, c_block = pieces
    cumulative = jnp.cumsum(step_block * decay_rate, axis=1)
    extent = step_block.shape[1]
    row_index = lax.broadcasted_iota(jnp.int32, (extent, extent), 0)
    col_index = lax.broadcasted_iota(jnp.int32, (extent, extent), 1)
    causal = (row_index >= col_index)[None, :, :, None]
    gaps = cumulative[:, :, None, :] - cumulative[:, None, :, :]
    kernel = jnp.exp(jnp.where(causal, gaps, -1e30))
    scores = jnp.einsum("btn,bsn->bts", c_block, b_block, precision=PRECISE)
    mixing = kernel * scores[..., None] * step_block[:, None, :, :]
    inner = jnp.einsum("btsh,bshp->bthp", mixing, x_block, precision=PRECISE)
    carried = (
        jnp.einsum("btn,bhpn->bthp", c_block, state, precision=PRECISE)
        * jnp.exp(cumulative)[..., None]
    )
    tail_weight = jnp.exp(cumulative[:, -1:, :] - cumulative) * step_block
    fresh = jnp.einsum("bsh,bshp,bsn->bhpn", tail_weight, x_block, b_block, precision=PRECISE)
    state = jnp.exp(cumulative[:, -1, :])[:, :, None, None] * state + fresh
    return ((state, decay_rate), inner + carried)


def local_scan(x_part, step_sizes, b_matrix, c_matrix, decay_rate, skip_weight, start):
    batch_seqs, extent = (step_sizes.shape[0], step_sizes.shape[1])
    block_size = min(extent, 256)
    block_count = extent // block_size

    def split_blocks(values):
        shaped = values.reshape((batch_seqs, block_count, block_size) + values.shape[2:])
        return jnp.moveaxis(shaped, 1, 0)

    carry_out, outputs = lax.scan(
        jax.checkpoint(stretch_update),
        (start, decay_rate),
        (
            split_blocks(x_part),
            split_blocks(step_sizes),
            split_blocks(b_matrix),
            split_blocks(c_matrix),
        ),
    )
    mixed = jnp.moveaxis(outputs, 0, 1).reshape(x_part.shape) + skip_weight[:, None] * x_part
    return mixed, carry_out[0]


def entering(growth, state, members, backward):
    count = lax.axis_size("seq")
    runs = count // members
    mine = lax.axis_index("seq") // members
    step = -members if backward else members
    pairs = [(i, i + step) for i in range(count) if 0 <= i + step < count]
    total = jnp.zeros_like(state)
    for _ in range(runs - 1):
        total = lax.ppermute(growth * total + state, "seq", pairs)
    return total


def orthogonal_rows(matrix, row_start, row_count):
    gram = jnp.dot(matrix, matrix.T, precision=PRECISE)
    gram = sum_over(gram, "head")
    size = jnp.trace(gram)
    factor = 1.0 / (jnp.sqrt(size) + 1e-07)
    gram = gram * (factor * factor)
    eye = jnp.eye(gram.shape[0], dtype=F32)
    polys = []
    for iteration in range(NS_STEPS):
        square = jnp.dot(gram, gram, precision=PRECISE)
        poly = COEF_A * eye + COEF_B * gram + COEF_C * square
        polys.append(poly)
        if iteration + 1 < NS_STEPS:
            image = COEF_A * gram + COEF_B * square
            image = image + COEF_C * jnp.dot(square, gram, precision=PRECISE)
            gram = jnp.dot(image, poly, precision=PRECISE)
    rows = lax.dynamic_slice_in_dim(polys[-1], row_start, row_count, 0)
    for poly in polys[-2::-1]:
        rows = jnp.dot(rows, poly, precision=PRECISE)
    return jnp.dot(rows, matrix, precision=PRECISE) * factor


def per_device(
    inputs,
    lengths,
    norm_gain,
    in_proj,
    conv_weight,
    conv_bias,
    head_params,
    gate_gain,
    out_proj,
    cotangent,
    norm_gain_mom,
    in_proj_mom,
    conv_weight_mom,
    conv_bias_mom,
    head_params_mom,
    gate_gain_mom,
    out_proj_mom,
):
    members, extent, model_width = inputs.shape
    seq_count = lax.axis_size("seq")
    head_count = lax.axis_size("head")
    seq_place = lax.axis_index("seq")
    head_place = lax.axis_index("head")
    heads_here = head_params.shape[1]
    head_span = gate_gain.shape[0]
    head_size = head_span // heads_here
    channels = conv_bias.shape[0]
    state_size = (channels - head_span) * head_count // 2
    inner_all = head_span * head_count
    group_cols = in_proj.shape[1]
    proj_all = group_cols * head_count
    tap_count = conv_weight.shape[0]
    share = model_width // seq_count
    tokens = members * extent
    quarter = extent // head_count
    runs = seq_count // members

    def to_sequence(blocks):
        piece = lax.dynamic_slice_in_dim(blocks, head_place * quarter, quarter, 1)
        piece = spread(piece, members)
        return piece, gather_head(piece, 1).reshape(tokens, -1)

    def from_sequence(piece):
        return gather_head(spread(piece.astype(BF), members), 1).reshape(inputs.shape)

    def own(per_token):
        return pick(per_token.reshape((members, head_count, quarter, -1)), head_place, 1)

    data_piece, data = to_sequence(inputs)
    cot_piece, cot = to_sequence(cotangent)
    data_piece, data = data_piece.astype(F32), data.astype(F32)
    run_place = seq_place // members
    positions = run_place * tokens + lax.broadcasted_iota(jnp.int32, (tokens, 1), 0)
    valid_mask = (positions < lengths[seq_place % members]).astype(F32)
    root_scale = lax.rsqrt(jnp.mean(data * data, axis=-1, keepdims=True) + EPSILON)
    normed = data * root_scale
    lowered = (normed * norm_gain).astype(BF)
    in_low = in_proj.astype(BF)
    projected = jnp.dot(lowered, in_low, preferred_element_type=F32)
    z_part = projected[:, :head_span]
    conv_in = projected[:, head_span : head_span + channels].astype(BF)
    raw_steps = projected[:, head_span + channels :]
    halo = tap_count - 1

    def from_run(edge, step):
        if runs == 1:
            return jnp.zeros_like(edge)
        pairs = [(i, i + step) for i in range(seq_count) if 0 <= i + step < seq_count]
        return lax.ppermute(edge, "seq", pairs)

    padded = jnp.concatenate([from_run(conv_in[tokens - halo :], members), conv_in], axis=0)
    conv_out = conv_bias + jnp.zeros(conv_in.shape, F32)
    for offset in range(tap_count):
        conv_out = conv_out + conv_weight[offset] * padded[offset : offset + tokens]
    activated = silu(conv_out)
    x_heads = activated[:, :head_span].reshape(1, tokens, heads_here, head_size)
    bc_local = activated[:, head_span:].astype(BF)
    bc_full = gather_head(bc_local.T, 0).reshape(2 * state_size, tokens).T.astype(F32)
    b_matrix = bc_full[None, :, :state_size]
    c_matrix = bc_full[None, :, state_size:]
    pre_steps = raw_steps + head_params[0]
    step_sizes = jax.nn.softplus(pre_steps)
    decay_rate = -jnp.exp(head_params[1])
    growth = jnp.exp(jnp.sum(step_sizes, axis=0) * decay_rate)[None, :, None, None]
    start = jnp.zeros((1, heads_here, head_size, state_size), F32)
    scan_args = (x_heads, step_sizes[None], b_matrix, c_matrix, decay_rate, head_params[2])
    if runs > 1:
        start = entering(growth, local_scan(*scan_args, start)[1], members, False)
    (mixed, state_end), pullback = jax.vjp(local_scan, *scan_args, start)
    mixed_flat = mixed.reshape(tokens, head_span)
    gate_value = silu(z_part)
    gated = mixed_flat * gate_value
    squares = jnp.sum(gated * gated, axis=-1)
    gated_low = (gated * gate_gain).astype(BF)
    out_low = out_proj.astype(BF)
    partial_out = jnp.dot(gated_low, out_low, preferred_element_type=F32)
    back_grad = cot.astype(F32) * valid_mask
    partial_scale = jnp.sum(back_grad * partial_out, axis=-1)
    square_sum, grad_scale = sum_over(jnp.stack([squares, partial_scale]), "head")
    norm_scale = lax.rsqrt(square_sum / inner_all + EPSILON)[:, None]
    grad_scale = grad_scale[:, None]
    summed = scatter_head(partial_out.reshape(members, head_count, quarter, -1), 1, BF)
    result = own(valid_mask) * (data_piece + own(norm_scale) * summed)
    output = from_sequence(result)
    result_squares = jnp.sum(result * result)
    grad_summed = (norm_scale * back_grad).astype(BF)
    grad_low = jnp.dot(grad_summed, out_low.T, preferred_element_type=F32)
    grad_gated = (
        grad_low * gate_gain - grad_scale * norm_scale * norm_scale * norm_scale * gated / inner_all
    )
    gate_gain_grad = jnp.sum(grad_low * gated, axis=0)
    grad_mixed = (grad_gated * gate_value).reshape(x_heads.shape)
    grad_z = grad_gated * mixed_flat * silu_slope(z_part)
    state_back = jnp.zeros_like(state_end)
    if runs > 1:
        state_back = entering(growth, pullback((grad_mixed, state_back))[6], members, True)
    grad_x, grad_steps, grad_b, grad_c, grad_rate, grad_skip, _ = pullback((grad_mixed, state_back))
    grad_bc = jnp.concatenate([grad_b[0], grad_c[0]], axis=-1).T
    grad_bc_local = scatter_head(grad_bc.reshape(head_count, -1, tokens), 0, F32).T
    grad_pre = grad_steps[0] * jax.nn.sigmoid(pre_steps)
    head_params_grad = jnp.stack([jnp.sum(grad_pre, axis=0), grad_rate * decay_rate, grad_skip])
    grad_activated = jnp.concatenate([grad_x.reshape(tokens, head_span), grad_bc_local], axis=-1)
    grad_conv = (grad_activated * silu_slope(conv_out)).astype(BF)
    trailing = jnp.concatenate([grad_conv, from_run(grad_conv[:halo], -members)], axis=0)
    grad_conv_wide = grad_conv.astype(F32)
    grad_conv_in = jnp.zeros(conv_in.shape, F32)
    tap_grads = []
    for offset in range(tap_count):
        lead = tap_count - 1 - offset
        grad_conv_in = grad_conv_in + conv_weight[offset] * trailing[lead : lead + tokens]
        tap_grads.append(jnp.sum(grad_conv_wide * padded[offset : offset + tokens], axis=0))
    conv_weight_grad = jnp.stack(tap_grads)
    conv_bias_grad = jnp.sum(grad_conv_wide, axis=0)
    grad_projected = jnp.concatenate([grad_z, grad_conv_in, grad_pre], axis=-1).astype(BF)
    partial_in = jnp.dot(grad_projected, in_low.T, preferred_element_type=F32)
    grad_lowered = scatter_head(partial_in.reshape(members, head_count, quarter, -1), 1, BF)
    root_piece = own(root_scale)
    normed_piece = data_piece * root_piece
    norm_gain_grad = jnp.sum(grad_lowered * normed_piece, axis=(0, 1))
    grad_normed = grad_lowered * norm_gain
    input_grad = own(back_grad) + root_piece * (
        grad_normed - normed_piece * jnp.mean(grad_normed * normed_piece, axis=-1, keepdims=True)
    )
    input_grad = from_sequence(input_grad).astype(F32)
    term_in = jnp.dot(lowered.T, grad_projected, preferred_element_type=F32)
    term_out = jnp.dot(grad_summed.T, gated_low, preferred_element_type=F32)
    out_grad_rows = lax.psum_scatter(term_out, "seq", scatter_dimension=0, tiled=True)
    in_proj_grad = lax.psum_scatter(term_in, "seq", scatter_dimension=0, tiled=True)
    norm_gain_grad, result_squares = sum_over((norm_gain_grad, result_squares), "head")
    (
        norm_gain_grad,
        conv_weight_grad,
        conv_bias_grad,
        head_params_grad,
        gate_gain_grad,
        squares_all,
    ) = sum_over(
        (
            norm_gain_grad,
            conv_weight_grad,
            conv_bias_grad,
            head_params_grad,
            gate_gain_grad,
            result_squares,
        ),
        "seq",
    )
    rms = jnp.sqrt(squares_all / (jnp.sum(lengths).astype(F32) * model_width))
    in_proj_mom_new = 0.5 * in_proj_mom + in_proj_grad
    out_rows_mom = 0.5 * out_proj_mom.T + out_grad_rows
    full_out = lax.all_gather(out_rows_mom, "seq", axis=0, tiled=True)
    full_in = lax.all_gather(in_proj_mom_new, "seq", axis=0, tiled=True)
    rows_out = orthogonal_rows(full_out, seq_place * share, share)
    rows_in = orthogonal_rows(full_in, seq_place * share, share)
    in_old_rows = lax.dynamic_slice_in_dim(in_proj, seq_place * share, share, 0)
    in_proj_new = in_old_rows - MUON_RATE * 0.2 * math.sqrt(max(model_width, proj_all)) * rows_in
    out_old_cols = lax.dynamic_slice_in_dim(out_proj, seq_place * share, share, 1)
    out_proj_new = (
        out_old_cols - MUON_RATE * 0.2 * math.sqrt(max(inner_all, model_width)) * rows_out.T
    )
    divisor = math.sqrt(members * extent * seq_count)
    norm_gain_mom_new = 0.5 * norm_gain_mom + norm_gain_grad
    conv_weight_mom_new = 0.5 * conv_weight_mom + conv_weight_grad
    conv_bias_mom_new = 0.5 * conv_bias_mom + conv_bias_grad
    head_params_mom_new = 0.5 * head_params_mom + head_params_grad
    gate_gain_mom_new = 0.5 * gate_gain_mom + gate_gain_grad
    norm_gain_new = norm_gain - SMALL_RATE * norm_gain_mom_new / divisor
    conv_weight_new = conv_weight - SMALL_RATE * conv_weight_mom_new / divisor
    conv_bias_new = conv_bias - SMALL_RATE * conv_bias_mom_new / divisor
    head_params_new = head_params - SMALL_RATE * head_params_mom_new / divisor
    gate_gain_new = gate_gain - SMALL_RATE * gate_gain_mom_new / divisor
    return (
        output,
        input_grad,
        norm_gain_grad,
        in_proj_grad,
        conv_weight_grad,
        conv_bias_grad,
        head_params_grad,
        gate_gain_grad,
        out_grad_rows.T,
        norm_gain_mom_new,
        in_proj_mom_new,
        conv_weight_mom_new,
        conv_bias_mom_new,
        head_params_mom_new,
        gate_gain_mom_new,
        out_rows_mom.T,
        norm_gain_new,
        in_proj_new,
        conv_weight_new,
        conv_bias_new,
        head_params_new,
        gate_gain_new,
        out_proj_new,
        rms,
    )


def solution(mesh):
    return jax.shard_map(
        per_device,
        mesh=mesh,
        in_specs=(
            P(None, "seq", None),
            P(),
            P(),
            P(None, "head"),
            P(None, "head"),
            P("head"),
            P(None, "head"),
            P("head"),
            P("head", None),
            P(None, "seq", None),
            P(),
            P("seq", "head"),
            P(None, "head"),
            P("head"),
            P(None, "head"),
            P("head"),
            P("head", "seq"),
        ),
        out_specs=(
            P(None, "seq", None),
            P(None, "seq", None),
            P(),
            P("seq", "head"),
            P(None, "head"),
            P("head"),
            P(None, "head"),
            P("head"),
            P("head", "seq"),
            P(),
            P("seq", "head"),
            P(None, "head"),
            P("head"),
            P(None, "head"),
            P("head"),
            P("head", "seq"),
            P(),
            P("seq", "head"),
            P(None, "head"),
            P("head"),
            P(None, "head"),
            P("head"),
            P("head", "seq"),
            P(),
        ),
        check_vma=False,
    )
```

time: 2190 us -> 1220 us (0.56)
  waiting for transfers between devices: 1650 us -> 246 us
  local copies, waits for them, and re-layouts: 50.5 us -> 311 us
  matrix products: 238 us -> 358 us
  blocking collectives: 83 us -> 0 us
  starting transfers between devices: 8.68 us -> 72.9 us
  other arithmetic: 135 us -> 196 us
    all_gather x23 -> x2, waiting for transfers between devices: 1140 us -> 0.02 us  [the longest x1 0.02 us: per_device(): full_out = lax.all_gather(out_rows_mom, 'seq', axis=0, tiled=True)]
    psum x7 -> x0, waiting for transfers between devices: 505 us -> none  [the longest x1 149 us: per_device(): whole_sum = lax.psum(whole_term, 'seq')]
    dynamic_update_slice x0 -> x56, local copies, waits for them, and re-layouts: none -> 170 us  [local_scan(): lax.scan(jax.checkpoint(stretch_update), (start, decay_rate), (split_bloc...]
    ppermute x2 -> x49, waiting for transfers between devices: 3.09 us -> 156 us  [flip(): return lax.ppermute(value, axis, [(i, i ^ bit) for i in range(count)])]
    dot_general x39 -> x44, matrix products: 160 us -> 233 us  [the longest x10 59 us: orthogonal_rows(): square = jnp.dot(gram, gram, precision=PRECISE)]
    all_to_all x0 -> x4, waiting for transfers between devices: none -> 58.3 us  [spread(): lax.all_to_all(blocks, 'seq', 0, 0, tiled=True, axis_index_groups=runs if...]
    another operation x13 -> x77, other arithmetic: 42.6 us -> 94.4 us
    psum x3 -> x0, blocking collectives: 51.7 us -> none  [the longest x1 38.7 us: per_device(): lax.psum((norm_gain_grad, conv_weight_grad, conv_bias_grad, head_params_g...]
  transfers between devices with their start and end apart: 33 -> 57, of which waited for: 30 -> 22; matrix products, arithmetic and copies ran while one was open for 10% -> 19% of each run, Pallas kernels for 0% -> 0%
where the time goes in v1:
time: 1220 us; the launch traced here: 1210 us
  matrix products  358 us (29%)
  local copies, waits for them, and re-layouts  311 us (25%)
  waiting for transfers between devices  246 us (20%)
  other arithmetic  196 us (16%)
  starting transfers between devices  72.9 us (6%)
  between operations  22.5 us (2%)
    dynamic_update_slice x56, local copies, waits for them, and re-layouts, local_scan(): lax.scan(jax.checkpoint(stretch_update), (start, decay_rate), (split_bloc...  170 us
    ppermute x49, waiting for transfers between devices, flip(): return lax.ppermute(value, axis, [(i, i ^ bit) for i in range(count)])  156 us
    another operation x57, other arithmetic  93.9 us
    dot_general x10, matrix products, orthogonal_rows(): square = jnp.dot(gram, gram, precision=PRECISE)  59 us
    all_to_all x4, waiting for transfers between devices, spread(): lax.all_to_all(blocks, 'seq', 0, 0, tiled=True, axis_index_groups=runs if...  58.3 us
    dot_general x8, matrix products, orthogonal_rows(): gram = jnp.dot(image, poly, precision=PRECISE)  56.9 us
    dot_general x24, matrix products, stretch_update(): inner = jnp.einsum('btsh,bshp->bthp', mixing, x_block, precision=PRECISE)  54.3 us
    ppermute x49, starting transfers between devices, flip(): return lax.ppermute(value, axis, [(i, i ^ bit) for i in range(count)])  53.9 us
  transfers between devices with their start and end apart: 57, of which 22 were waited for; matrix products, arithmetic and copies ran while one was open for 19% of the time, Pallas kernels for 0%

profile of v1, /device:TPU:0, one launch (start us, length us, event | category | flops | bytes accessed | tf_op | source)
XLA Modules:
  0.0 1211.3 jit_solution(3379281210585016213)
XLA Ops:
  19.5 18.1 %all-to-all-done = bf16[8,64,768]{2,1,0:T(8,128)(2,1)S(1)} async-done(((bf16[8,64,768]{2,1,0:T(8,128)(2,1)}), bf16[8,64,768]{2,1,0:T(8,128)(2,1)S(1)}, u32[]{:S(2)}, u32[]{:S(2)}) %all-to-all-start) | async-done | bytes 786464 | tf_op jit(solution)/shard_map/all_to_all | solution.py:72
  42.8 18.8 %all-to-all-done.1 = bf16[8,64,768]{2,1,0:T(8,128)(2,1)S(1)} async-done(((bf16[8,64,768]{2,1,0:T(8,128)(2,1)}), bf16[8,64,768]{2,1,0:T(8,128)(2,1)S(1)}, u32[]{:S(2)}, u32[]{:S(2)}) %all-to-all-start.1) | async-done | bytes 786464 | tf_op jit(solution)/shard_map/all_to_all | solution.py:72
  65.1 14.6 %collective-permute-done.7 = bf16[8,64,768]{2,1,0:T(8,128)(2,1)} collective-permute-done((bf16[8,64,768]{2,1,0:T(8,128)(2,1)S(1)}, bf16[8,64,768]{2,1,0:T(8,128)(2,1)}, u32[]{:S(2)}, u32[]{:S(2)}) %collective-permute-start.7) | collective-permute-done | bytes 786464 | tf_op jit(solution)/shard_map/ppermute | solution.py:31
  127.2 167.8 %while.43 = (s32[]{:T(128)}, f32[1,6,64,128]{3,2,1,0:T(8,128)S(1)}, f32[8,1,256,6,64]{2,0,4,3,1:T(8,128)}, f32[8,1,6,64,128]{4,3,2,1,0:T(8,128)}, f32[8,6]{1,0:T...) while((s32[]{:T(128)}, f32[1,6,64,128]{3,2,1,0:T(8,128)S(1)}, ...), condition=%wide.region_4.5_spmd.clone, body=%wide.region_1.4_spmd.clone.sunk | while | flops 706957824 | bytes 5812649 | solution.py:109
  136.2 9.8 dynamic_update_slice.75
  157.1 9.8 dynamic_update_slice.75
  178.0 9.8 dynamic_update_slice.75
  198.9 9.8 dynamic_update_slice.75
  219.8 9.8 dynamic_update_slice.75
  240.7 9.8 dynamic_update_slice.75
  261.6 9.8 dynamic_update_slice.75
  282.6 9.8 dynamic_update_slice.75
  336.4 304.9 %while.44 = (s32[]{:T(128)}, f32[1,6,64,128]{3,2,1,0:T(8,128)S(1)}, f32[6]{0:T(128)S(1)}, f32[8,1,256,6,64]{2,0,4,3,1:T(8,128)}, f32[8,1,256,6]{3,2,1,0:T(8,128)...) while((s32[]{:T(128)}, f32[1,6,64,128]{3,2,1,0:T(8,128)S(1)}, ...), condition=%wide.region_20.21_spmd.clone, body=%wide.region_7.20_spmd.clone.sunk | while | flops 1669247488 | bytes 15689316 | solution.py:109
  364.3 9.8 dynamic_update_slice.80
  402.4 9.8 dynamic_update_slice.80
  440.5 9.8 dynamic_update_slice.80
  478.6 9.8 dynamic_update_slice.80
  516.7 9.8 dynamic_update_slice.80
  554.8 9.8 dynamic_update_slice.80
  592.9 9.8 dynamic_update_slice.80
  631.0 9.8 dynamic_update_slice.80
  673.2 9.8 collective-permute-done.17
  698.9 31.7 %reduce-scatter.5.cloned.1.call-done = f32[96,384]{1,0:T(8,128)} async-done(((f32[768,384]{1,0:T(8,128)}), f32[96,384]{1,0:T(8,128)}) %reduce-scatter.5.cloned.1.call-update) | async-done | bytes 147472 | tf_op jit(solution)/shard_map/reduce_scatter | solution.py:304
  750.9 14.0 %collective-permute-done.12 = bf16[8,64,768]{2,1,0:T(8,128)(2,1)} collective-permute-done((bf16[8,64,768]{2,1,0:T(8,128)(2,1)}, bf16[8,64,768]{2,1,0:T(8,128)(2,1)}, u32[]{:S(2)}, u32[]{:S(2)}) %collective-permute-start.12) | collective-permute-done | bytes 786464 | tf_op jit(solution)/shard_map/ppermute | solution.py:31
  764.9 14.1 %collective-permute-done.19 = bf16[8,64,768]{2,1,0:T(8,128)(2,1)} collective-permute-done((bf16[8,64,768]{2,1,0:T(8,128)(2,1)}, bf16[8,64,768]{2,1,0:T(8,128)(2,1)}, u32[]{:S(2)}, u32[]{:S(2)}) %collective-permute-start.19) | collective-permute-done | bytes 786464 | tf_op jit(solution)/shard_map/ppermute | solution.py:31
  804.5 21.5 %all-to-all-done.3 = bf16[8,64,768]{2,1,0:T(8,128)(2,1)S(1)} async-done(((bf16[8,64,768]{2,1,0:T(8,128)(2,1)}), bf16[8,64,768]{2,1,0:T(8,128)(2,1)S(1)}, u32[]{:S(2)}, u32[]{:S(2)}) %all-to-all-start.3) | async-done | bytes 786464 | tf_op jit(solution)/shard_map/all_to_all | solution.py:72
  863.5 10.1 collective-permute-start.45
  903.9 50.8 %collective-permute-done.14 = bf16[8,64,768]{2,1,0:T(8,128)(2,1)} collective-permute-done((bf16[8,64,768]{2,1,0:T(8,128)(2,1)}, bf16[8,64,768]{2,1,0:T(8,128)(2,1)}, u32[]{:S(2)}, u32[]{:S(2)}) %collective-permute-start.14) | collective-permute-done | bytes 786464 | tf_op jit(solution)/shard_map/ppermute | solution.py:31
  984.2 8.9 fusion.151
  1007.9 10.5 fusion.426
  1080.7 28.6 %collective-permute-done.41 = f32[768,768]{1,0:T(8,128)S(1)} collective-permute-done((f32[768,768]{1,0:T(8,128)S(1)}, f32[768,768]{1,0:T(8,128)S(1)}, u32[]{:S(2)}, u32[]{:S(2)}) %collective-permute-start.41) | collective-permute-done | bytes 2359328 | tf_op jit(solution)/shard_map/ppermute | solution.py:31
  1122.8 8.7 fusion.175
  (1014 shorter events, 768.0 us)
Async XLA Ops:
  10.0 27.6 %all-to-all-start = ((bf16[8,64,768]{2,1,0:T(8,128)(2,1)}), bf16[8,64,768]{2,1,0:T(8,128)(2,1)S(1)}, u32[]{:S(2)}, u32[]{:S(2)}) async-start(bf16[8,64,768]{2,1,0:T(8,128)(2,1)} %constant_dynamic-slice_fusion.13), calls=%async_computation | async-start | bytes 1572864 | tf_op jit(solution)/shard_map/all_to_all | solution.py:72
  37.6 23.9 %all-to-all-start.1 = ((bf16[8,64,768]{2,1,0:T(8,128)(2,1)}), bf16[8,64,768]{2,1,0:T(8,128)(2,1)S(1)}, u32[]{:S(2)}, u32[]{:S(2)}) async-start(bf16[8,64,768]{2,1,0:T(8,128)(2,1)} %constant_dynamic-slice_fusion.12), calls=%async_computation.1 | async-start | bytes 1572864 | tf_op jit(solution)/shard_map/all_to_all | solution.py:72
  41.2 689.4 %reduce-scatter.5.cloned.1.call-start = ((), (), s32[]{:S(2)}) async-start(), calls=%async_computation.7 | async-start | bytes 1327104 | tf_op jit(solution)/shard_map/reduce_scatter | solution.py:304
  41.2 23.2 %collective-permute-start.1 = (bf16[8,64,768]{2,1,0:T(8,128)(2,1)S(1)}, bf16[8,64,768]{2,1,0:T(8,128)(2,1)}, u32[]{:S(2)}, u32[]{:S(2)}) collective-permute-start(bf16[8,64,768]{2,1,0:T(8,128)(2,1)S(1)} %all-to-all-done), channel_id=1, source_target_pairs={{0,2},{1,3},{2,0},{3,1},{4,6},{5,7},{6,4},{7,5},{8,10},{9,11},{10,... | collective-permute-start | bytes 2359304 | tf_op jit(solution)/shard_map/ppermute | solution.py:31
  61.5 18.2 %collective-permute-start.7 = (bf16[8,64,768]{2,1,0:T(8,128)(2,1)S(1)}, bf16[8,64,768]{2,1,0:T(8,128)(2,1)}, u32[]{:S(2)}, u32[]{:S(2)}) collective-permute-start(bf16[8,64,768]{2,1,0:T(8,128)(2,1)S(1)} %all-to-all-done.1), channel_id=1, source_target_pairs={{0,2},{1,3},{2,0},{3,1},{4,6},{5,7},{6,4},{7,5},{8,10},{9,11},{10,... | collective-permute-start | bytes 2359304 | tf_op jit(solution)/shard_map/ppermute | solution.py:31
  63.1 16.7 %collective-permute-start.6 = (bf16[8,64,768]{2,1,0:T(8,128)(2,1)S(1)}, bf16[8,64,768]{2,1,0:T(8,128)(2,1)}, u32[]{:S(2)}, u32[]{:S(2)}) collective-permute-start(bf16[8,64,768]{2,1,0:T(8,128)(2,1)S(1)} %all-to-all-done.1), channel_id=1, source_target_pairs={{0,1},{1,0},{2,3},{3,2},{4,5},{5,4},{6,7},{7,6},{8,9},{9,8},{10,11... | collective-permute-start | bytes 2359304 | tf_op jit(solution)/shard_map/ppermute | solution.py:31
  63.1 19.6 %collective-permute-start = (bf16[8,64,768]{2,1,0:T(8,128)(2,1)S(1)}, bf16[8,64,768]{2,1,0:T(8,128)(2,1)S(1)}, u32[]{:S(2)}, u32[]{:S(2)}) collective-permute-start(bf16[8,64,768]{2,1,0:T(8,128)(2,1)S(1)} %all-to-all-done), channel_id=1, source_target_pairs={{0,1},{1,0},{2,3},{3,2},{4,5},{5,4},{6,7},{7,6},{8,9},{9,8},{10,11... | collective-permute-start | bytes 2359304 | tf_op jit(solution)/shard_map/ppermute | solution.py:31
  64.4 18.7 %collective-permute-start.2 = (bf16[8,64,768]{2,1,0:T(8,128)(2,1)}, bf16[8,64,768]{2,1,0:T(8,128)(2,1)S(1)}, u32[]{:S(2)}, u32[]{:S(2)}) collective-permute-start(bf16[8,64,768]{2,1,0:T(8,128)(2,1)} %collective-permute-done.1), channel_id=1, source_target_pairs={{0,1},{1,0},{2,3},{3,2},{4,5},{5,4},{6,7},{7,6},{8,9},{9,8},{10,11... | collective-permute-start | bytes 2359304 | tf_op jit(solution)/shard_map/ppermute | solution.py:31
  79.7 24.2 %collective-permute-start.8 = (bf16[8,64,768]{2,1,0:T(8,128)(2,1)}, bf16[8,64,768]{2,1,0:T(8,128)(2,1)}, u32[]{:S(2)}, u32[]{:S(2)}) collective-permute-start(bf16[8,64,768]{2,1,0:T(8,128)(2,1)} %collective-permute-done.7), channel_id=1, source_target_pairs={{0,1},{1,0},{2,3},{3,2},{4,5},{5,4},{6,7},{7,6},{8,9},{9,8},{10,11... | collective-permute-start | bytes 2359304 | tf_op jit(solution)/shard_map/ppermute | solution.py:31
  101.7 17.4 %collective-permute-start.3 = (bf16[64,2048]{1,0:T(8,128)(2,1)S(1)}, bf16[64,2048]{1,0:T(8,128)(2,1)S(1)}, u32[]{:S(2)}, u32[]{:S(2)}) collective-permute-start(bf16[64,2048]{1,0:T(8,128)(2,1)S(1)} %get-tuple-element.777), channel_id=1, source_target_pairs={{0,1},{1,0},{2,3},{3,2},{4,5},{5,4},{6,7},{7,6},{8,9},{9,8},{10,11... | collective-permute-start | bytes 786440 | tf_op jit(solution)/shard_map/ppermute | solution.py:31
  647.9 19.5 %collective-permute-start.16 = (f32[2,64,2048]{2,1,0:T(8,128)}, f32[2,64,2048]{2,1,0:T(8,128)}, u32[]{:S(2)}, u32[]{:S(2)}) collective-permute-start(f32[2,64,2048]{2,1,0:T(8,128)} %dynamic-slice_bitcast_fusion.5), channel_id=1, source_target_pairs={{0,1},{1,0},{2,3},{3,2},{4,5},{5,4},{6,7},{7,6},{8,9},{9,8},{10,11... | collective-permute-start | bytes 3145736 | tf_op jit(solution)/shard_map/ppermute | solution.py:31
  655.5 85.0 %collective-permute-start.11 = (f32[8,2,64,768]{3,2,0,1:T(8,128)}, f32[8,2,64,768]{3,2,0,1:T(8,128)}, u32[]{:S(2)}, u32[]{:S(2)}) collective-permute-start(f32[8,2,64,768]{3,2,0,1:T(8,128)} %bitcast.477), channel_id=1, source_target_pairs={{0,1},{1,0},{2,3},{3,2},{4,5},{5,4},{6,7},{7,6},{8,9},{9,8},{10,11... | collective-permute-start | bytes 9437192 | tf_op jit(solution)/shard_map/ppermute | solution.py:31
  666.1 124.5 %all-gather.5.cloned.1.call-start = ((), (), s32[]{:S(2)}) async-start(), calls=%async_computation.9 | async-start | bytes 1327104 | tf_op jit(solution)/shard_map/all_gather | solution.py:328
  698.9 46.8 %collective-permute-start.18 = (f32[8,2,64,768]{3,2,0,1:T(8,128)}, f32[8,2,64,768]{3,2,0,1:T(8,128)}, u32[]{:S(2)}, u32[]{:S(2)}) collective-permute-start(f32[8,2,64,768]{3,2,0,1:T(8,128)} %bitcast.476), channel_id=1, source_target_pairs={{0,1},{1,0},{2,3},{3,2},{4,5},{5,4},{6,7},{7,6},{8,9},{9,8},{10,11... | collective-permute-start | bytes 9437192 | tf_op jit(solution)/shard_map/ppermute | solution.py:31
  732.2 166.5 %reduce-scatter.3.cloned.1.call-start = ((), (), s32[]{:S(2)}) async-start(), calls=%async_computation.6 | async-start | bytes 3096576 | tf_op jit(solution)/shard_map/reduce_scatter | solution.py:305
  744.1 20.8 %collective-permute-start.12 = (bf16[8,64,768]{2,1,0:T(8,128)(2,1)}, bf16[8,64,768]{2,1,0:T(8,128)(2,1)}, u32[]{:S(2)}, u32[]{:S(2)}) collective-permute-start(bf16[8,64,768]{2,1,0:T(8,128)(2,1)} %fusion.308), channel_id=1, source_target_pairs={{0,2},{1,3},{2,0},{3,1},{4,6},{5,7},{6,4},{7,5},{8,10},{9,11},{10,... | collective-permute-start | bytes 2359304 | tf_op jit(solution)/shard_map/ppermute | solution.py:31
  749.0 30.1 %collective-permute-start.19 = (bf16[8,64,768]{2,1,0:T(8,128)(2,1)}, bf16[8,64,768]{2,1,0:T(8,128)(2,1)}, u32[]{:S(2)}, u32[]{:S(2)}) collective-permute-start(bf16[8,64,768]{2,1,0:T(8,128)(2,1)} %fusion.309), channel_id=1, source_target_pairs={{0,2},{1,3},{2,0},{3,1},{4,6},{5,7},{6,4},{7,5},{8,10},{9,11},{10,... | collective-permute-start | bytes 2359304 | tf_op jit(solution)/shard_map/ppermute | solution.py:31
  787.0 39.0 %all-to-all-start.3 = ((bf16[8,64,768]{2,1,0:T(8,128)(2,1)}), bf16[8,64,768]{2,1,0:T(8,128)(2,1)S(1)}, u32[]{:S(2)}, u32[]{:S(2)}) async-start(bf16[8,64,768]{2,1,0:T(8,128)(2,1)} %fusion.225), calls=%async_computation.3 | async-start | bytes 1572864 | tf_op jit(solution)/shard_map/all_to_all | solution.py:72
  796.2 84.1 %collective-permute-start.42 = (f32[768,768]{1,0:T(8,128)S(1)}, f32[768,768]{1,0:T(8,128)}, u32[]{:S(2)}, u32[]{:S(2)}) collective-permute-start(f32[768,768]{1,0:T(8,128)S(1)} %fusion.434), channel_id=1, source_target_pairs={{0,1},{1,0},{2,3},{3,2},{4,5},{5,4},{6,7},{7,6},{8,9},{9,8},{10,11... | collective-permute-start | bytes 7077896 | tf_op jit(solution)/shard_map/ppermute | solution.py:31
  825.9 65.1 %all-to-all-start.2 = ((bf16[8,64,768]{2,1,0:T(8,128)(2,1)}), bf16[8,64,768]{2,1,0:T(8,128)(2,1)}, u32[]{:S(2)}, u32[]{:S(2)}) async-start(bf16[8,64,768]{2,1,0:T(8,128)(2,1)} %get-tuple-element.775), calls=%async_computation.2 | async-start | bytes 1572864 | tf_op jit(solution)/shard_map/all_to_all | solution.py:72
  830.1 177.8 %all-gather.3.cloned.1.call-start = ((), (), s32[]{:S(2)}) async-start(), calls=%async_computation.8 | async-start | bytes 3096576 | tf_op jit(solution)/shard_map/all_gather | solution.py:329
  857.0 44.2 %collective-permute-start.21 = (bf16[8,64,768]{2,1,0:T(8,128)(2,1)S(1)}, bf16[8,64,768]{2,1,0:T(8,128)(2,1)}, u32[]{:S(2)}, u32[]{:S(2)}) collective-permute-start(bf16[8,64,768]{2,1,0:T(8,128)(2,1)S(1)} %all-to-all-done.3), channel_id=1, source_target_pairs={{0,2},{1,3},{2,0},{3,1},{4,6},{5,7},{6,4},{7,5},{8,10},{9,11},{10,... | collective-permute-start | bytes 2359304 | tf_op jit(solution)/shard_map/ppermute | solution.py:31
  859.7 26.4 %collective-permute-start.39 = (f32[384]{0:T(512)S(1)}, f32[384]{0:T(512)}, u32[]{:S(2)}, u32[]{:S(2)}) collective-permute-start(f32[384]{0:T(512)S(1)} %add.559), channel_id=1, source_target_pairs={{0,16},{4,20},{8,24},{12,28},{16,0},{20,4},{24,8},{28,12},{1,17},{... | collective-permute-start | bytes 4616 | tf_op jit(solution)/shard_map/ppermute | solution.py:31
  860.6 30.4 %collective-permute-start.26 = (f32[768]{0:T(1024)S(1)}, f32[768]{0:T(1024)}, u32[]{:S(2)}, u32[]{:S(2)}) collective-permute-start(f32[768]{0:T(1024)S(1)} %add.546), channel_id=1, source_target_pairs={{0,8},{4,12},{8,0},{12,4},{16,24},{20,28},{24,16},{28,20},{1,9},{5... | collective-permute-start | bytes 9224 | tf_op jit(solution)/shard_map/ppermute | solution.py:31
  880.3 15.7 %collective-permute-start.30 = (f32[4,448]{1,0:T(4,128)S(1)}, f32[4,448]{1,0:T(4,128)S(1)}, u32[]{:S(2)}, u32[]{:S(2)}) collective-permute-start(f32[4,448]{1,0:T(4,128)S(1)} %fusion.494), channel_id=1, source_target_pairs={{0,16},{4,20},{8,24},{12,28},{16,0},{20,4},{24,8},{28,12},{1,17},{... | collective-permute-start | bytes 21512 | tf_op jit(solution)/shard_map/ppermute | solution.py:31
  889.6 78.9 %collective-permute-start.43 = (f32[768,768]{1,0:T(8,128)}, f32[768,768]{1,0:T(8,128)}, u32[]{:S(2)}, u32[]{:S(2)}) collective-permute-start(f32[768,768]{1,0:T(8,128)} %add.590), channel_id=1, source_target_pairs={{0,2},{1,3},{2,0},{3,1},{4,6},{5,7},{6,4},{7,5},{8,10},{9,11},{10,... | collective-permute-start | bytes 7077896 | tf_op jit(solution)/shard_map/ppermute | solution.py:31
  891.0 63.7 %collective-permute-start.14 = (bf16[8,64,768]{2,1,0:T(8,128)(2,1)}, bf16[8,64,768]{2,1,0:T(8,128)(2,1)}, u32[]{:S(2)}, u32[]{:S(2)}) collective-permute-start(bf16[8,64,768]{2,1,0:T(8,128)(2,1)} %all-to-all-done.2), channel_id=1, source_target_pairs={{0,2},{1,3},{2,0},{3,1},{4,6},{5,7},{6,4},{7,5},{8,10},{9,11},{10,... | collective-permute-start | bytes 2359304 | tf_op jit(solution)/shard_map/ppermute | solution.py:31
  898.7 56.6 %collective-permute-start.20 = (bf16[8,64,768]{2,1,0:T(8,128)(2,1)S(1)}, bf16[8,64,768]{2,1,0:T(8,128)(2,1)S(1)}, u32[]{:S(2)}, u32[]{:S(2)}) collective-permute-start(bf16[8,64,768]{2,1,0:T(8,128)(2,1)S(1)} %all-to-all-done.3), channel_id=1, source_target_pairs={{0,1},{1,0},{2,3},{3,2},{4,5},{5,4},{6,7},{7,6},{8,9},{9,8},{10,11... | collective-permute-start | bytes 2359304 | tf_op jit(solution)/shard_map/ppermute | solution.py:31
  900.6 54.9 %collective-permute-start.13 = (bf16[8,64,768]{2,1,0:T(8,128)(2,1)}, bf16[8,64,768]{2,1,0:T(8,128)(2,1)}, u32[]{:S(2)}, u32[]{:S(2)}) collective-permute-start(bf16[8,64,768]{2,1,0:T(8,128)(2,1)} %all-to-all-done.2), channel_id=1, source_target_pairs={{0,1},{1,0},{2,3},{3,2},{4,5},{5,4},{6,7},{7,6},{8,9},{9,8},{10,11... | collective-permute-start | bytes 2359304 | tf_op jit(solution)/shard_map/ppermute | solution.py:31
  901.2 56.5 %collective-permute-start.22 = (bf16[8,64,768]{2,1,0:T(8,128)(2,1)}, bf16[8,64,768]{2,1,0:T(8,128)(2,1)}, u32[]{:S(2)}, u32[]{:S(2)}) collective-permute-start(bf16[8,64,768]{2,1,0:T(8,128)(2,1)} %collective-permute-done.21), channel_id=1, source_target_pairs={{0,1},{1,0},{2,3},{3,2},{4,5},{5,4},{6,7},{7,6},{8,9},{9,8},{10,11... | collective-permute-start | bytes 2359304 | tf_op jit(solution)/shard_map/ppermute | solution.py:31
  1018.4 37.3 %collective-permute-start.40 = (f32[768,768]{1,0:T(8,128)S(1)}, f32[768,768]{1,0:T(8,128)S(1)}, u32[]{:S(2)}, u32[]{:S(2)}) collective-permute-start(f32[768,768]{1,0:T(8,128)S(1)} %fusion.426), channel_id=1, source_target_pairs={{0,1},{1,0},{2,3},{3,2},{4,5},{5,4},{6,7},{7,6},{8,9},{9,8},{10,11... | collective-permute-start | bytes 7077896 | tf_op jit(solution)/shard_map/ppermute | solution.py:31
  1056.1 53.2 %collective-permute-start.41 = (f32[768,768]{1,0:T(8,128)S(1)}, f32[768,768]{1,0:T(8,128)S(1)}, u32[]{:S(2)}, u32[]{:S(2)}) collective-permute-start(f32[768,768]{1,0:T(8,128)S(1)} %add.569), channel_id=1, source_target_pairs={{0,2},{1,3},{2,0},{3,1},{4,6},{5,7},{6,4},{7,5},{8,10},{9,11},{10,... | collective-permute-start | bytes 7077896 | tf_op jit(solution)/shard_map/ppermute | solution.py:31
  (86 other events, 868.0 us)
Sparse Core Ops, SparseCore 0:
  666.2 64.3 reduce-scatter.4
  733.3 40.0 all-gather.4
  777.5 91.8 reduce-scatter.2
  900.7 54.4 all-gather.2

commit v2 on v1

v2 whole, which is shorter than its diff:
```python
import functools
import math

import jax
import jax.numpy as jnp
from jax import lax
from jax.experimental import pallas as pl
from jax.experimental.pallas import tpu as pltpu
from jax.sharding import PartitionSpec as P

NS_STEPS = 5
EPSILON = 1e-05
COEF_A = 3.4445
COEF_B = -4.775
COEF_C = 2.0315
MUON_RATE = 0.2
SMALL_RATE = 0.2
PRECISE = lax.Precision.HIGHEST
BF = jnp.bfloat16
F32 = jnp.float32


def silu(values):
    return values * jax.nn.sigmoid(values)


def silu_slope(values):
    sigmoid_value = jax.nn.sigmoid(values)
    return sigmoid_value * (1.0 + values * (1.0 - sigmoid_value))


def flip(value, axis, bit):
    count = lax.axis_size(axis)
    return lax.ppermute(value, axis, [(i, i ^ bit) for i in range(count)])


def sum_over(value, axis):
    bit = 1
    while bit < lax.axis_size(axis):
        value = jax.tree.map(lambda part: part + flip(part, axis, bit), value)
        bit *= 2
    return value


def pick(stacked, index, axis):
    return lax.dynamic_index_in_dim(stacked, index, axis, keepdims=False)


def gather_head(piece, axis):
    place = lax.axis_index("head")
    across = flip(piece, "head", 2)
    beside = flip(piece, "head", 1)
    corner = flip(across, "head", 1)
    low, high = place % 2, place // 2
    near = jnp.where(low == 0, jnp.stack([piece, beside], axis), jnp.stack([beside, piece], axis))
    far = jnp.where(low == 0, jnp.stack([across, corner], axis), jnp.stack([corner, across], axis))
    return jnp.where(
        high == 0, jnp.concatenate([near, far], axis), jnp.concatenate([far, near], axis)
    )


def scatter_head(parts, axis, wire):
    place = lax.axis_index("head")
    low, high = place % 2, place // 2
    shape = parts.shape
    parts = parts.reshape(shape[:axis] + (2, 2) + shape[axis + 1 :])
    half = pick(parts, low, axis + 1) + flip(pick(parts, 1 - low, axis + 1), "head", 1)
    sent = flip(pick(half, 1 - high, axis).astype(wire), "head", 2)
    return pick(half, high, axis) + sent.astype(F32)


def spread(blocks, members):
    count = lax.axis_size("seq")
    runs = [list(range(i, i + members)) for i in range(0, count, members)]
    return lax.all_to_all(
        blocks, "seq", 0, 0, tiled=True, axis_index_groups=runs if len(runs) > 1 else None
    )


def entering(growth, state, members, backward):
    count = lax.axis_size("seq")
    runs = count // members
    mine = lax.axis_index("seq") // members
    step = -members if backward else members
    pairs = [(i, i + step) for i in range(count) if 0 <= i + step < count]
    total = jnp.zeros_like(state)
    for _ in range(runs - 1):
        total = lax.ppermute(growth * total + state, "seq", pairs)
    return total


CHUNK = 128
LANES = 128
SUBLANES = 8
VMEM_BYTES = 56 * 1024 * 1024


def split(values, terms):
    pieces = []
    for _ in range(terms):
        pieces.append(values.astype(BF))
        values = values - pieces[-1].astype(F32)
    return pieces


def product(left, right, dims=((1,), (0,))):
    total = None
    for i, a in enumerate(left):
        for j, b in enumerate(right):
            if i + j < max(len(left), len(right)):
                part = lax.dot_general(a, b, (dims, ((), ())), preferred_element_type=F32)
                total = part if total is None else total + part
    return total


ROWS_OF_BOTH = ((1,), (1,))


def columns(rows):
    count, extent = rows.shape
    return jnp.concatenate([rows, jnp.zeros((LANES - count, extent), F32)], axis=0).T


def lane_pair(left, right, half):
    lane = lax.broadcasted_iota(jnp.int32, (CHUNK, LANES), 1)
    return jnp.where(lane < half, left, right)


def apart(pair, half):
    lane = lax.broadcasted_iota(jnp.int32, pair.shape, 1)
    zero = jnp.zeros_like(pair)
    return jnp.concatenate([jnp.where(lane < half, pair, zero), jnp.where(lane < half, zero, pair)], 0)


def head_sums(values, half):
    lane = lax.broadcasted_iota(jnp.int32, values.shape, 1)
    first = jnp.sum(jnp.where(lane < half, values, 0.0), axis=1, keepdims=True)
    return first, jnp.sum(values, axis=1, keepdims=True) - first


def forward_kernel(
    half, terms, place_ref, conv_ref, z_ref, c_ref, bt_ref, rows_ref, skip_ref, gain_ref,
    out_low_ref, cot_ref, start_ref,
    mixed_ref, states_ref, end_ref, gated_ref, partial_ref, sums_ref, state_ref,
):
    step = pl.program_id(0)
    block = conv_ref.shape[0]
    span = conv_ref.shape[1]
    pairs = span // LANES

    @pl.when(step == 0)
    def _():
        state_ref[...] = start_ref[...]

    causal = lax.broadcasted_iota(jnp.int32, (CHUNK, CHUNK), 0) >= lax.broadcasted_iota(
        jnp.int32, (CHUNK, CHUNK), 1
    )
    for sub in range(block // CHUNK):
        here = slice(sub * CHUNK, (sub + 1) * CHUNK)
        rows = rows_ref[:, here]
        cols = columns(rows)
        c_block, bt_block = c_ref[here], bt_ref[:, here]
        scores = product([c_block], [bt_block])
        states_ref[sub] = state_ref[...]
        state_parts = split(state_ref[...], terms)
        carried = product([c_block], state_parts)
        weighted, grown = [], []
        for pair in range(pairs):
            lanes = slice(pair * LANES, (pair + 1) * LANES)
            first, second = 2 * pair, 2 * pair + 1
            x = silu(conv_ref[here, lanes])

            def pair_cols(table, offset):
                return lane_pair(
                    table[:, offset + first : offset + first + 1],
                    table[:, offset + second : offset + second + 1],
                    half,
                )

            cum = pair_cols(cols, SUBLANES)
            scaled = x * pair_cols(cols, 0)
            last = cum[CHUNK - 1 : CHUNK]
            growth = jnp.exp(cum)
            weighted.append(scaled * jnp.exp(last - cum))
            grown.append(growth[CHUNK - 1 : CHUNK])
            mixing = []
            for head in (first, second):
                gap = cols[:, SUBLANES + head : SUBLANES + head + 1] - rows[SUBLANES + head : SUBLANES + head + 1]
                mixing.append(jnp.exp(jnp.where(causal, gap, -1e30)) * scores)
            inner = product(
                split(jnp.concatenate(mixing, axis=1), terms), split(apart(scaled, half), terms)
            )
            mixed_ref[here, lanes] = inner + carried[:, lanes] * growth + skip_ref[:, lanes] * x
        fresh = product([bt_block], split(jnp.concatenate(weighted, axis=1), terms))
        state_ref[...] = jnp.concatenate(grown, axis=1) * state_ref[...] + fresh
    end_ref[...] = state_ref[...]
    gated = mixed_ref[...] * silu(z_ref[...])
    gated_low = (gated * gain_ref[...]).astype(BF)
    gated_ref[...] = gated_low
    partial = jnp.dot(gated_low, out_low_ref[...], preferred_element_type=F32)
    partial_ref[...] = partial.reshape(partial_ref.shape).astype(partial_ref.dtype)
    squares = jnp.sum(gated * gated, axis=1, keepdims=True)
    slot = place_ref[1] + step * block + lax.broadcasted_iota(jnp.int32, (block, 1), 0)
    back = jnp.where(slot < place_ref[0], cot_ref[...].astype(F32), 0.0)
    scale = jnp.sum(back * partial, axis=1, keepdims=True)
    lane = lax.broadcasted_iota(jnp.int32, (block, LANES), 1)
    sums = jnp.where(lane == 0, squares, jnp.where(lane == 1, scale, 0.0))
    for sub in range(block // CHUNK):
        here = slice(sub * CHUNK, (sub + 1) * CHUNK)
        sums_ref[:, here] = sums[here].T[:SUBLANES]


def forward_scan(place, conv, z, c_mat, bt, rows, skip, gain, out_low, cot, start, half, members, parts):
    tokens, span = conv.shape
    width = cot.shape[1]
    state = c_mat.shape[1]
    block = tokens // members
    subs = block // CHUNK
    by_rows = lambda i, *_: (i, 0)
    by_lanes = lambda i, *_: (0, i)
    whole = lambda i, *_: (0, 0)
    quarter = block // parts
    return pl.pallas_call(
        functools.partial(forward_kernel, half, 2),
        grid_spec=pltpu.PrefetchScalarGridSpec(
            num_scalar_prefetch=1,
            grid=(members,),
            in_specs=[
                pl.BlockSpec((block, span), by_rows),
                pl.BlockSpec((block, span), by_rows),
                pl.BlockSpec((block, state), by_rows),
                pl.BlockSpec((state, block), by_lanes),
                pl.BlockSpec((2 * SUBLANES, block), by_lanes),
                pl.BlockSpec((1, span), whole),
                pl.BlockSpec((1, span), whole),
                pl.BlockSpec((span, width), whole),
                pl.BlockSpec((block, width), by_rows),
                pl.BlockSpec((state, span), whole),
            ],
            out_specs=[
                pl.BlockSpec((block, span), by_rows),
                pl.BlockSpec((subs, state, span), lambda i, *_: (i, 0, 0)),
                pl.BlockSpec((state, span), whole),
                pl.BlockSpec((block, span), by_rows),
                pl.BlockSpec((parts, 1, quarter, width), lambda i, *_: (0, i, 0, 0)),
                pl.BlockSpec((SUBLANES, block), by_lanes),
            ],
            scratch_shapes=[pltpu.VMEM((state, span), F32)],
        ),
        out_shape=[
            jax.ShapeDtypeStruct((tokens, span), F32),
            jax.ShapeDtypeStruct((tokens // CHUNK, state, span), F32),
            jax.ShapeDtypeStruct((state, span), F32),
            jax.ShapeDtypeStruct((tokens, span), BF),
            jax.ShapeDtypeStruct((parts, members, quarter, width), F32),
            jax.ShapeDtypeStruct((SUBLANES, tokens), F32),
        ],
        compiler_params=pltpu.CompilerParams(vmem_limit_bytes=VMEM_BYTES),
    )(place, conv, z, c_mat, bt, rows, skip, gain, out_low, cot, start)


def gate_kernel(
    inner_all, place_ref, cot_ref, norm_ref, z_ref, mixed_ref, gain_ref, out_turned_ref,
    grad_mixed_ref, grad_z_ref, grad_summed_ref, gain_grad_ref,
):
    step = pl.program_id(0)
    block = cot_ref.shape[0]
    norm = jnp.concatenate(
        [columns(norm_ref[:, sub * CHUNK : (sub + 1) * CHUNK]) for sub in range(block // CHUNK)], 0
    )
    norm_scale, grad_scale = norm[:, 0:1], norm[:, 1:2]
    slot = place_ref[1] + step * block + lax.broadcasted_iota(jnp.int32, (block, 1), 0)
    back = jnp.where(slot < place_ref[0], cot_ref[...].astype(F32), 0.0)
    grad_summed = (norm_scale * back).astype(BF)
    grad_summed_ref[...] = grad_summed
    grad_low = jnp.dot(grad_summed, out_turned_ref[...], preferred_element_type=F32)
    z, mixed = z_ref[...], mixed_ref[...]
    sigmoid = jax.nn.sigmoid(z)
    gate = z * sigmoid
    gated = mixed * gate
    shrink = grad_scale * norm_scale * norm_scale * norm_scale / inner_all
    grad_gated = grad_low * gain_ref[...] - shrink * gated
    grad_mixed_ref[...] = grad_gated * gate
    grad_z_ref[...] = (grad_gated * mixed * (sigmoid * (1.0 + z * (1.0 - sigmoid)))).astype(BF)

    @pl.when(step == 0)
    def _():
        gain_grad_ref[...] = jnp.zeros_like(gain_grad_ref)

    gain_grad_ref[...] += jnp.sum(grad_low * gated, axis=0, keepdims=True)


def gate_back(place, cot, norm_rows, z, mixed, gain, out_turned, inner_all, members):
    tokens, span = z.shape
    width = cot.shape[1]
    block = tokens // members
    by_rows = lambda i, *_: (i, 0)
    whole = lambda i, *_: (0, 0)
    return pl.pallas_call(
        functools.partial(gate_kernel, inner_all),
        grid_spec=pltpu.PrefetchScalarGridSpec(
            num_scalar_prefetch=1,
            grid=(members,),
            in_specs=[
                pl.BlockSpec((block, width), by_rows),
                pl.BlockSpec((SUBLANES, block), lambda i, *_: (0, i)),
                pl.BlockSpec((block, span), by_rows),
                pl.BlockSpec((block, span), by_rows),
                pl.BlockSpec((1, span), whole),
                pl.BlockSpec((width, span), whole),
            ],
            out_specs=[
                pl.BlockSpec((block, span), by_rows),
                pl.BlockSpec((block, span), by_rows),
                pl.BlockSpec((block, width), by_rows),
                pl.BlockSpec((1, span), whole),
            ],
        ),
        out_shape=[
            jax.ShapeDtypeStruct((tokens, span), F32),
            jax.ShapeDtypeStruct((tokens, span), BF),
            jax.ShapeDtypeStruct((tokens, width), BF),
            jax.ShapeDtypeStruct((1, span), F32),
        ],
        compiler_params=pltpu.CompilerParams(vmem_limit_bytes=VMEM_BYTES),
    )(place, cot, norm_rows, z, mixed, gain, out_turned)


def backward_kernel(
    half, terms, taps, grad_ref, conv_ref, conv_in_ref, b_ref, c_ref, bt_ref, ct_ref, rows_ref, states_ref,
    end_ref, skip_ref, weight_ref, back_ref, halo_ref,
    grad_x_ref, grad_bc_ref, rows_out_ref, first_ref, edge_ref, small_ref,
    carry_ref, after_ref, shift_ref,
):
    step = pl.program_id(0)
    block = conv_ref.shape[0]
    span = conv_ref.shape[1]
    pairs = span // LANES
    state = b_ref.shape[1]
    subs = block // CHUNK

    @pl.when(step == 0)
    def _():
        carry_ref[...] = back_ref[...]
        after_ref[...] = end_ref[...]
        shift_ref[:SUBLANES] = halo_ref[...]
        small_ref[...] = jnp.zeros_like(small_ref)

    row = lax.broadcasted_iota(jnp.int32, (CHUNK, CHUNK), 0)
    lane = lax.broadcasted_iota(jnp.int32, (CHUNK, CHUNK), 1)
    causal = row <= lane
    for sub in reversed(range(subs)):
        here = slice(sub * CHUNK, (sub + 1) * CHUNK)
        rows = rows_ref[:, here]
        cols = columns(rows)
        b_block, c_block, bt_block, ct_block = b_ref[here], c_ref[here], bt_ref[:, here], ct_ref[:, here]
        scores = product([b_block], [ct_block])
        entered = states_ref[sub]
        carry = carry_ref[...]
        entered_parts = split(entered, terms)
        carry_parts = split(carry, terms)
        carried = product([c_block], entered_parts)
        pulled = product([b_block], carry_parts)
        joint = jnp.sum(carry * after_ref[...], axis=0, keepdims=True)
        after_ref[...] = entered
        head_of = lax.broadcasted_iota(jnp.int32, (SUBLANES, span), 1) // half
        joint = jnp.sum(
            jnp.where(head_of == lax.broadcasted_iota(jnp.int32, (SUBLANES, span), 0), joint, 0.0),
            axis=1,
            keepdims=True,
        )
        weighted, grown_grad, grown = [], [], []
        grad_scores = jnp.zeros((CHUNK, CHUNK), F32)
        col_sums = jnp.zeros((CHUNK, LANES), F32)
        row_sums = []
        for pair in range(pairs):
            lanes = slice(pair * LANES, (pair + 1) * LANES)
            first, second = 2 * pair, 2 * pair + 1

            def pair_cols(offset):
                return lane_pair(
                    cols[:, offset + first : offset + first + 1],
                    cols[:, offset + second : offset + second + 1],
                    half,
                )

            conv = conv_ref[here, lanes]
            sigmoid = jax.nn.sigmoid(conv)
            x = conv * sigmoid
            grad = grad_ref[here, lanes]
            cum, size = pair_cols(SUBLANES), pair_cols(0)
            scaled = x * size
            last = cum[CHUNK - 1 : CHUNK]
            growth = jnp.exp(cum)
            tail = jnp.exp(last - cum)
            weighted.append(scaled * tail)
            grown_grad.append(grad * growth)
            grown.append(growth[CHUNK - 1 : CHUNK])
            grad_apart = split(apart(grad, half), terms)
            dots = product(split(scaled, terms), grad_apart, ROWS_OF_BOTH)
            kernels = []
            for k, head in enumerate((first, second)):
                gap = rows[SUBLANES + head : SUBLANES + head + 1] - cols[:, SUBLANES + head : SUBLANES + head + 1]
                decay = jnp.exp(jnp.where(causal, gap, -1e30))
                grad_score = decay * dots[:, k * CHUNK : (k + 1) * CHUNK]
                grad_scores = grad_scores + grad_score
                kernels.append(decay * scores)
                both = grad_score * scores
                row_sums.append(jnp.sum(both, axis=0, keepdims=True))
                col_sums = jnp.where(
                    lane == head, col_sums - jnp.sum(both, axis=1, keepdims=True), col_sums
                )
            pulled_pair = tail * pulled[:, lanes]
            force = product(split(jnp.concatenate(kernels, axis=1), terms), grad_apart) + pulled_pair
            grad_x = size * force + skip_ref[:, lanes] * grad
            flow = grown_grad[-1] * carried[:, lanes] - scaled * pulled_pair
            direct = x * force
            for head, flow_sum, direct_sum in zip(
                (first, second), head_sums(flow, half), head_sums(direct, half)
            ):
                col_sums = jnp.where(lane == head, col_sums + flow_sum, col_sums)
                col_sums = jnp.where(lane == SUBLANES + head, direct_sum, col_sums)
            small_ref[taps + 1 : taps + 2, lanes] += jnp.sum(grad * x, axis=0, keepdims=True)
            grad_conv = (grad_x * (sigmoid * (1.0 + conv * (1.0 - sigmoid)))).astype(BF).astype(F32)
            shift_ref[CHUNK : CHUNK + SUBLANES, lanes] = shift_ref[:SUBLANES, lanes]
            shift_ref[:CHUNK, lanes] = grad_conv
            conv_in = conv_in_ref[here, lanes].astype(F32)
            total = None
            for tap in range(taps):
                moved = shift_ref[taps - 1 - tap : taps - 1 - tap + CHUNK, lanes]
                term = weight_ref[tap : tap + 1, lanes] * moved
                total = term if total is None else total + term
                small_ref[tap : tap + 1, lanes] += jnp.sum(conv_in * moved, axis=0, keepdims=True)
            small_ref[taps : taps + 1, lanes] += jnp.sum(grad_conv, axis=0, keepdims=True)
            grad_x_ref[here, lanes] = total.astype(BF)
        grown_parts = split(jnp.concatenate(grown_grad, axis=1), terms)
        weighted_parts = split(jnp.concatenate(weighted, axis=1), terms)
        grad_b = product(carry_parts, weighted_parts, ROWS_OF_BOTH) + product(
            [ct_block], split(grad_scores.T, terms)
        )
        grad_c = product(entered_parts, grown_parts, ROWS_OF_BOTH) + product(
            [bt_block], split(grad_scores, terms)
        )
        grad_bc_ref[:state, here] = grad_b
        grad_bc_ref[state:, here] = grad_c
        carry_ref[...] = jnp.concatenate(grown, axis=1) * carry + product([ct_block], grown_parts)
        turned = col_sums.T
        row_sums.append(jnp.zeros((SUBLANES - 2 * pairs, CHUNK), F32))
        slots = lax.broadcasted_iota(jnp.int32, (SUBLANES, CHUNK), 1)
        rows_out_ref[:SUBLANES, here] = (
            jnp.concatenate(row_sums, axis=0)
            + turned[:SUBLANES]
            + jnp.where(slots == CHUNK - 1, joint, 0.0)
        )
        rows_out_ref[SUBLANES:, here] = turned[SUBLANES : 2 * SUBLANES]
    first_ref[...] = carry_ref[...]
    edge_ref[...] = shift_ref[:SUBLANES]


def backward_scan(grad, conv, conv_in, b_mat, c_mat, bt, ct, rows, states, end, skip, weight, back, halo, half, members):
    tokens, span = conv.shape
    state = b_mat.shape[1]
    taps = weight.shape[0]
    block = tokens // members
    subs = block // CHUNK
    final = members - 1
    by_rows = lambda i: (final - i, 0)
    by_lanes = lambda i: (0, final - i)
    whole = lambda i: (0, 0)
    return pl.pallas_call(
        functools.partial(backward_kernel, half, 2, taps),
        grid=(members,),
        in_specs=[
            pl.BlockSpec((block, span), by_rows),
            pl.BlockSpec((block, span), by_rows),
            pl.BlockSpec((block, span), by_rows),
            pl.BlockSpec((block, state), by_rows),
            pl.BlockSpec((block, state), by_rows),
            pl.BlockSpec((state, block), by_lanes),
            pl.BlockSpec((state, block), by_lanes),
            pl.BlockSpec((2 * SUBLANES, block), by_lanes),
            pl.BlockSpec((subs, state, span), lambda i: (final - i, 0, 0)),
            pl.BlockSpec((state, span), whole),
            pl.BlockSpec((1, span), whole),
            pl.BlockSpec((taps, span), whole),
            pl.BlockSpec((state, span), whole),
            pl.BlockSpec((SUBLANES, span), whole),
        ],
        out_specs=[
            pl.BlockSpec((block, span), by_rows),
            pl.BlockSpec((2 * state, block), by_lanes),
            pl.BlockSpec((2 * SUBLANES, block), by_lanes),
            pl.BlockSpec((state, span), whole),
            pl.BlockSpec((SUBLANES, span), whole),
            pl.BlockSpec((SUBLANES, span), whole),
        ],
        out_shape=[
            jax.ShapeDtypeStruct((tokens, span), BF),
            jax.ShapeDtypeStruct((2 * state, tokens), F32),
            jax.ShapeDtypeStruct((2 * SUBLANES, tokens), F32),
            jax.ShapeDtypeStruct((state, span), F32),
            jax.ShapeDtypeStruct((SUBLANES, span), F32),
            jax.ShapeDtypeStruct((SUBLANES, span), F32),
        ],
        scratch_shapes=[
            pltpu.VMEM((state, span), F32),
            pltpu.VMEM((state, span), F32),
            pltpu.VMEM((CHUNK + SUBLANES, span), F32),
        ],
        compiler_params=pltpu.CompilerParams(vmem_limit_bytes=VMEM_BYTES),
    )(grad, conv, conv_in, b_mat, c_mat, bt, ct, rows, states, end, skip, weight, back, halo)


def newton_kernel(gram_ref, pick_ref, rows_ref, gram, first, second, third, polys):
    width = gram_ref.shape[0]
    tile = 256
    tiles = [slice(i, i + tile) for i in range(0, width, tile)]

    def store(pair, here, values):
        high = values.astype(BF)
        pair[0, here] = high
        pair[1, here] = (values - high.astype(F32)).astype(BF)

    def times(left, here, right):
        high, low = left[0, here], left[1, here]
        total = jnp.dot(high, right[1], preferred_element_type=F32)
        total = total + jnp.dot(low, right[0], preferred_element_type=F32)
        return total + jnp.dot(high, right[0], preferred_element_type=F32)

    def eye(here):
        row = lax.broadcasted_iota(jnp.int32, (tile, width), 0) + here.start
        return row == lax.broadcasted_iota(jnp.int32, (tile, width), 1)

    size = jnp.zeros((1, 1), F32)
    for here in tiles:
        size = size + jnp.sum(jnp.where(eye(here), gram_ref[here], 0.0), keepdims=True)
    factor = 1.0 / (jnp.sqrt(size) + 1e-07)
    for here in tiles:
        gram[here] = gram_ref[here] * (factor * factor)
        store(first, here, gram[here])
    for step in range(NS_STEPS):
        for here in tiles:
            square = times(first, here, first)
            store(second, here, square)
            poly = jnp.where(eye(here), COEF_A, 0.0) + COEF_B * gram[here] + COEF_C * square
            store(polys.at[step], here, poly)
            gram[here] = COEF_A * gram[here] + COEF_B * square
        if step + 1 < NS_STEPS:
            for here in tiles:
                store(third, here, gram[here] + COEF_C * times(second, here, first))
            for here in tiles:
                gram[here] = times(third, here, polys.at[step])
            for here in tiles:
                store(first, here, gram[here])
    picked = pick_ref[...]
    last = polys.at[NS_STEPS - 1]
    rows = jnp.dot(picked, last[0], preferred_element_type=F32) + jnp.dot(
        picked, last[1], preferred_element_type=F32
    )
    for step in reversed(range(NS_STEPS - 1)):
        rows = product(split(rows, 2), [polys[step, 0], polys[step, 1]])
    rows_ref[...] = rows * factor


def newton_rows(gram, picked):
    width = gram.shape[0]
    pair = pltpu.VMEM((2, width, width), BF)
    return pl.pallas_call(
        newton_kernel,
        out_shape=jax.ShapeDtypeStruct(picked.shape, F32),
        in_specs=[pl.BlockSpec(memory_space=pltpu.VMEM)] * 2,
        out_specs=pl.BlockSpec(memory_space=pltpu.VMEM),
        scratch_shapes=[
            pltpu.VMEM((width, width), F32),
            pair,
            pair,
            pair,
            pltpu.VMEM((NS_STEPS, 2, width, width), BF),
        ],
        compiler_params=pltpu.CompilerParams(vmem_limit_bytes=VMEM_BYTES),
    )(gram, picked)


def whole_gram(pieces):
    gram = sum(
        jnp.dot(piece, piece.T, precision=lax.Precision.HIGH, preferred_element_type=F32)
        for piece in pieces
    )
    low = lax.axis_index("head") % 2
    halves = gram.reshape((2, -1) + gram.shape[1:])
    half = pick(halves, low, 0) + flip(pick(halves, 1 - low, 0), "head", 1)
    half = half + flip(half, "head", 2)
    other = flip(half, "head", 1)
    return jnp.concatenate(
        [jnp.where(low == 0, half, other), jnp.where(low == 0, other, half)], axis=0
    )


def per_device(
    inputs,
    lengths,
    norm_gain,
    in_proj,
    conv_weight,
    conv_bias,
    head_params,
    gate_gain,
    out_proj,
    cotangent,
    norm_gain_mom,
    in_proj_mom,
    conv_weight_mom,
    conv_bias_mom,
    head_params_mom,
    gate_gain_mom,
    out_proj_mom,
):
    members, extent, model_width = inputs.shape
    seq_count = lax.axis_size("seq")
    head_count = lax.axis_size("head")
    seq_place = lax.axis_index("seq")
    head_place = lax.axis_index("head")
    heads_here = head_params.shape[1]
    head_span = gate_gain.shape[0]
    head_size = head_span // heads_here
    channels = conv_bias.shape[0]
    state_size = (channels - head_span) * head_count // 2
    inner_all = head_span * head_count
    group_cols = in_proj.shape[1]
    proj_all = group_cols * head_count
    tap_count = conv_weight.shape[0]
    share = model_width // seq_count
    tokens = members * extent
    quarter = extent // head_count
    runs = seq_count // members

    def to_sequence(blocks):
        piece = lax.dynamic_slice_in_dim(blocks, head_place * quarter, quarter, 1)
        piece = spread(piece, members)
        return piece, gather_head(piece, 1).reshape(tokens, -1)

    def from_sequence(piece):
        return gather_head(spread(piece.astype(BF), members), 1).reshape(inputs.shape)

    def own(per_token):
        return pick(per_token.reshape((members, head_count, quarter, -1)), head_place, 1)

    data_piece, data = to_sequence(inputs)
    cot_piece, cot = to_sequence(cotangent)
    data_piece, data = data_piece.astype(F32), data.astype(F32)
    run_place = seq_place // members
    length = lengths[seq_place % members]
    first_slot = run_place * tokens
    place = jnp.stack([length, first_slot]).astype(jnp.int32)
    root_scale = lax.rsqrt(jnp.mean(data * data, axis=-1, keepdims=True) + EPSILON)
    lowered = (data * root_scale * norm_gain).astype(BF)
    in_low = in_proj.astype(BF)
    x_end = 2 * head_span
    bc_end = head_span + channels
    halo = tap_count - 1

    def from_run(edge, step):
        if runs == 1:
            return jnp.zeros_like(edge)
        pairs = [(i, i + step) for i in range(seq_count) if 0 <= i + step < seq_count]
        return lax.ppermute(edge, "seq", pairs)

    side = lax.dot_general(
        in_low[:, x_end:], lowered, (((0,), (1,)), ((), ())), preferred_element_type=F32
    )
    bc_in = side[: bc_end - x_end].astype(BF)
    bc_weight = conv_weight[:, head_span:, None]
    bc_padded = jnp.concatenate([from_run(bc_in[:, tokens - halo :], members), bc_in], axis=1)
    bc_conv = conv_bias[head_span:, None] + jnp.zeros(bc_in.shape, F32)
    for offset in range(tap_count):
        bc_conv = bc_conv + bc_weight[offset] * bc_padded[:, offset : offset + tokens]
    bc_full = gather_head(silu(bc_conv).astype(BF), 0).reshape(2, state_size, tokens)
    bt, ct = bc_full[0], bc_full[1]
    b_mat, c_mat = bt.T, ct.T
    pre_steps = side[bc_end - x_end :] + head_params[0][:, None]
    step_sizes = jax.nn.softplus(pre_steps)
    decay_rate = -jnp.exp(head_params[1])[:, None]
    chunk_row = lax.broadcasted_iota(jnp.int32, (CHUNK, CHUNK), 0)
    chunk_col = lax.broadcasted_iota(jnp.int32, (CHUNK, CHUNK), 1)
    upto = (chunk_row <= chunk_col).astype(F32)

    def chunk_dot(rows, matrix):
        return jnp.dot(rows.reshape(-1, CHUNK), matrix, precision=PRECISE).reshape(rows.shape)

    cumulative = chunk_dot(step_sizes * decay_rate, upto)
    spare = jnp.zeros((SUBLANES - heads_here, tokens), F32)
    rows = jnp.concatenate([step_sizes, spare, cumulative, spare], axis=0)
    growth = jnp.repeat(jnp.exp(jnp.sum(step_sizes * decay_rate, axis=1)), head_size)[None]

    z_part = jnp.dot(lowered, in_low[:, :head_span], preferred_element_type=F32)
    x_in = jnp.dot(lowered, in_low[:, head_span:x_end], preferred_element_type=F32).astype(BF)
    x_weight = conv_weight[:, :head_span]
    x_padded = jnp.concatenate([from_run(x_in[tokens - halo :], members), x_in], axis=0)
    x_conv = conv_bias[:head_span] + jnp.zeros(x_in.shape, F32)
    for offset in range(tap_count):
        x_conv = x_conv + x_weight[offset] * x_padded[offset : offset + tokens]

    skip = jnp.repeat(head_params[2], head_size)[None]
    gain = gate_gain[None]
    out_low = out_proj.astype(BF)

    def scan_from(start):
        return forward_scan(
            place, x_conv, z_part, c_mat, bt, rows, skip, gain, out_low, cot, start, head_size, members, head_count
        )

    start = jnp.zeros((state_size, head_span), F32)
    if runs > 1:
        start = entering(growth, scan_from(start)[2], members, False)
    mixed, states, state_end, gated_low, partial_out, sums = scan_from(start)
    square_sum, grad_scale = sum_over(sums[:2], "head")
    norm_scale = lax.rsqrt(square_sum / inner_all + EPSILON)
    norm_rows = jnp.concatenate(
        [norm_scale[None], grad_scale[None], jnp.zeros((SUBLANES - 2, tokens), F32)], axis=0
    )
    grad_mixed, grad_z, grad_summed, gate_gain_grad = gate_back(
        place, cot, norm_rows, z_part, mixed, gain, out_low.T, inner_all, members
    )
    gate_gain_grad = gate_gain_grad[0]

    def rows_of(term):
        return lax.psum_scatter(term, "seq", scatter_dimension=0, tiled=True)

    early = jnp.concatenate(
        [
            jnp.dot(lowered.T, grad_z, preferred_element_type=F32),
            jnp.dot(grad_summed.T, gated_low, preferred_element_type=F32),
        ],
        axis=1,
    )
    early_rows = rows_of(early)

    summed = scatter_head(partial_out, 0, BF)
    slots = first_slot + lax.broadcasted_iota(jnp.int32, (tokens, 1), 0)
    valid_mask = own((slots < length).astype(F32))
    result = valid_mask * (data_piece + own(norm_scale) * summed)
    output = from_sequence(result)
    result_squares = jnp.sum(result * result)

    def scan_back(back, edge):
        return backward_scan(
            grad_mixed, x_conv, x_in, b_mat, c_mat, bt, ct, rows, states, state_end, skip, x_weight,
            back, edge, head_size, members,
        )

    back = jnp.zeros_like(state_end)
    edge = jnp.zeros((SUBLANES, head_span), F32)
    if runs > 1:
        back = entering(growth, scan_back(back, edge)[3], members, True)
        edge = from_run(scan_back(back, edge)[4], -members)
    grad_x_in, grad_bc, grad_rows, _, _, small = scan_back(back, edge)
    grad_bc = scatter_head(grad_bc.reshape(head_count, -1, tokens), 0, F32)
    grad_cum, grad_direct = grad_rows[:heads_here], grad_rows[SUBLANES : SUBLANES + heads_here]
    grad_decay = chunk_dot(grad_cum, upto.T)
    grad_pre = (grad_direct + grad_decay * decay_rate) * jax.nn.sigmoid(pre_steps)
    head_params_grad = jnp.stack(
        [
            jnp.sum(grad_pre, axis=1),
            jnp.sum(grad_decay * step_sizes, axis=1) * decay_rate[:, 0],
            jnp.sum(small[tap_count + 1].reshape(heads_here, head_size), axis=1),
        ]
    )
    grad_conv = (grad_bc * silu_slope(bc_conv)).astype(BF)
    trailing = jnp.concatenate([grad_conv, from_run(grad_conv[:, :halo], -members)], axis=1)
    grad_bc_in = jnp.zeros(bc_in.shape, F32)
    tap_grads = []
    for offset in range(tap_count):
        lead = halo - offset
        moved = trailing[:, lead : lead + tokens].astype(F32)
        grad_bc_in = grad_bc_in + bc_weight[offset] * moved
        tap_grads.append(jnp.sum(moved * bc_in, axis=1))
    conv_weight_grad = jnp.concatenate([small[:tap_count], jnp.stack(tap_grads)], axis=1)
    conv_bias_grad = jnp.concatenate([small[tap_count], jnp.sum(grad_conv.astype(F32), axis=1)])
    grad_side = jnp.concatenate([grad_bc_in, grad_pre], axis=0).astype(BF).T
    grad_late = jnp.concatenate([grad_x_in, grad_side], axis=1)
    late_rows = rows_of(jnp.dot(lowered.T, grad_late, preferred_element_type=F32))
    in_proj_grad = jnp.concatenate([early_rows[:, :head_span], late_rows], axis=1)
    out_grad_rows = early_rows[:, head_span:]
    partial_in = jnp.dot(
        jnp.concatenate([grad_z, grad_late], axis=1), in_low.T, preferred_element_type=F32
    )
    grad_lowered = scatter_head(partial_in.reshape(members, head_count, quarter, -1), 1, BF)
    root_piece = own(root_scale)
    normed_piece = data_piece * root_piece
    norm_gain_grad = jnp.sum(grad_lowered * normed_piece, axis=(0, 1))
    grad_normed = grad_lowered * norm_gain
    input_grad = valid_mask * cot_piece.astype(F32) + root_piece * (
        grad_normed - normed_piece * jnp.mean(grad_normed * normed_piece, axis=-1, keepdims=True)
    )
    input_grad = from_sequence(input_grad).astype(F32)
    norm_gain_grad, result_squares = sum_over((norm_gain_grad, result_squares), "head")
    small_parts = (
        norm_gain_grad,
        conv_weight_grad,
        conv_bias_grad,
        head_params_grad,
        gate_gain_grad,
        result_squares,
    )
    packed = sum_over(jnp.concatenate([part.reshape(-1) for part in small_parts]), "seq")
    unpacked = []
    for part in small_parts:
        unpacked.append(packed[: part.size].reshape(part.shape))
        packed = packed[part.size :]
    (
        norm_gain_grad,
        conv_weight_grad,
        conv_bias_grad,
        head_params_grad,
        gate_gain_grad,
        squares_all,
    ) = unpacked
    rms = jnp.sqrt(squares_all / (jnp.sum(lengths).astype(F32) * model_width))
    in_proj_mom_new = 0.5 * in_proj_mom + in_proj_grad
    out_rows_mom = 0.5 * out_proj_mom.T + out_grad_rows
    def whole(rows):
        return lax.all_gather(rows, "seq", axis=0, tiled=True)

    early_whole = whole(jnp.concatenate([in_proj_mom_new[:, :head_span], out_rows_mom], axis=1))
    late_whole = whole(in_proj_mom_new[:, head_span:])
    full_out = early_whole[:, head_span:]
    full_in = early_whole[:, :head_span]
    picked_rows = -(-share // (2 * SUBLANES)) * 2 * SUBLANES
    picked = seq_place * share + lax.broadcasted_iota(jnp.int32, (picked_rows, model_width), 0)
    picked = (picked == lax.broadcasted_iota(jnp.int32, picked.shape, 1)).astype(BF)
    turn_out = newton_rows(whole_gram([full_out]), picked)[:share]
    turn_in = newton_rows(whole_gram([full_in, late_whole]), picked)[:share]

    def turned(turn, matrix):
        return jnp.dot(turn, matrix, precision=lax.Precision.HIGH, preferred_element_type=F32)

    rows_out = turned(turn_out, full_out)
    rows_in = jnp.concatenate([turned(turn_in, full_in), turned(turn_in, late_whole)], axis=1)
    in_old_rows = lax.dynamic_slice_in_dim(in_proj, seq_place * share, share, 0)
    in_proj_new = in_old_rows - MUON_RATE * 0.2 * math.sqrt(max(model_width, proj_all)) * rows_in
    out_old_cols = lax.dynamic_slice_in_dim(out_proj, seq_place * share, share, 1)
    out_proj_new = (
        out_old_cols - MUON_RATE * 0.2 * math.sqrt(max(inner_all, model_width)) * rows_out.T
    )
    divisor = math.sqrt(members * extent * seq_count)
    norm_gain_mom_new = 0.5 * norm_gain_mom + norm_gain_grad
    conv_weight_mom_new = 0.5 * conv_weight_mom + conv_weight_grad
    conv_bias_mom_new = 0.5 * conv_bias_mom + conv_bias_grad
    head_params_mom_new = 0.5 * head_params_mom + head_params_grad
    gate_gain_mom_new = 0.5 * gate_gain_mom + gate_gain_grad
    norm_gain_new = norm_gain - SMALL_RATE * norm_gain_mom_new / divisor
    conv_weight_new = conv_weight - SMALL_RATE * conv_weight_mom_new / divisor
    conv_bias_new = conv_bias - SMALL_RATE * conv_bias_mom_new / divisor
    head_params_new = head_params - SMALL_RATE * head_params_mom_new / divisor
    gate_gain_new = gate_gain - SMALL_RATE * gate_gain_mom_new / divisor
    return (
        output,
        input_grad,
        norm_gain_grad,
        in_proj_grad,
        conv_weight_grad,
        conv_bias_grad,
        head_params_grad,
        gate_gain_grad,
        out_grad_rows.T,
        norm_gain_mom_new,
        in_proj_mom_new,
        conv_weight_mom_new,
        conv_bias_mom_new,
        head_params_mom_new,
        gate_gain_mom_new,
        out_rows_mom.T,
        norm_gain_new,
        in_proj_new,
        conv_weight_new,
        conv_bias_new,
        head_params_new,
        gate_gain_new,
        out_proj_new,
        rms,
    )


def solution(mesh):
    return jax.shard_map(
        per_device,
        mesh=mesh,
        in_specs=(
            P(None, "seq", None),
            P(),
            P(),
            P(None, "head"),
            P(None, "head"),
            P("head"),
            P(None, "head"),
            P("head"),
            P("head", None),
            P(None, "seq", None),
            P(),
            P("seq", "head"),
            P(None, "head"),
            P("head"),
            P(None, "head"),
            P("head"),
            P("head", "seq"),
        ),
        out_specs=(
            P(None, "seq", None),
            P(None, "seq", None),
            P(),
            P("seq", "head"),
            P(None, "head"),
            P("head"),
            P(None, "head"),
            P("head"),
            P("head", "seq"),
            P(),
            P("seq", "head"),
            P(None, "head"),
            P("head"),
            P(None, "head"),
            P("head"),
            P("head", "seq"),
            P(),
            P("seq", "head"),
            P(None, "head"),
            P("head"),
            P(None, "head"),
            P("head"),
            P("head", "seq"),
            P(),
        ),
        check_vma=False,
    )
```

time: 1220 us -> 661 us (0.54)
  matrix products: 358 us -> 37.4 us
  local copies, waits for them, and re-layouts: 311 us -> 57.4 us
  Pallas kernels: 0 us -> 146 us
  other arithmetic: 196 us -> 86 us
  starting transfers between devices: 72.9 us -> 45.6 us
  waiting for transfers between devices: 246 us -> 264 us
    dot_general x156 -> x14, matrix products: 358 us -> 32.8 us  [the longest x3 11.3 us: whole_gram(): jnp.dot(piece, piece.T, precision=lax.Precision.HIGH, preferred_element_t...]
    dynamic_update_slice x56 -> x0, local copies, waits for them, and re-layouts: 170 us -> none  [local_scan(): lax.scan(jax.checkpoint(stretch_update), (start, decay_rate), (split_bloc...]
    pallas_call x0 -> x5, Pallas kernels: none -> 146 us  [the longest x2 93.3 us: newton_rows(): pl.pallas_call(newton_kernel, out_shape=jax.ShapeDtypeStruct(picked.shape...]
    another operation x77 -> x2, other arithmetic: 94.1 us -> 1.24 us  [the longest x1 1.23 us: per_device(): place = jnp.stack([length, first_slot]).astype(jnp.int32)]
    reduce_scatter x2, waiting for transfers between devices: 31.7 us -> 73.7 us  [rows_of(): return lax.psum_scatter(term, 'seq', scatter_dimension=0, tiled=True)]
    ppermute x49 -> x36, waiting for transfers between devices: 156 us -> 118 us  [flip(): return lax.ppermute(value, axis, [(i, i ^ bit) for i in range(count)])]
    all_gather x2, waiting for transfers between devices: 0.02 us -> 35.6 us  [whole(): return lax.all_gather(rows, 'seq', axis=0, tiled=True)]
    squeeze x40 -> x0, local copies, waits for them, and re-layouts: 31.4 us -> none  [local_scan(): lax.scan(jax.checkpoint(stretch_update), (start, decay_rate), (split_bloc...]
  transfers between devices with their start and end apart: 57 -> 44, of which waited for: 22 -> 21; matrix products, arithmetic and copies ran while one was open for 19% -> 23% of each run, Pallas kernels for 0% -> 11%
where the time goes in v2:
time: 661 us; the launch traced here: 656 us
  waiting for transfers between devices  264 us (40%)
  Pallas kernels  146 us (22%)
  other arithmetic  86 us (13%)
  local copies, waits for them, and re-layouts  57.4 us (9%)
  starting transfers between devices  45.6 us (7%)
  matrix products  37.4 us (6%)
  between operations  19.5 us (3%)
    ppermute x36, waiting for transfers between devices, flip(): return lax.ppermute(value, axis, [(i, i ^ bit) for i in range(count)])  118 us
    pallas_call x2, Pallas kernels, newton_rows(): pl.pallas_call(newton_kernel, out_shape=jax.ShapeDtypeStruct(picked.shape...  93.3 us
    reduce_scatter x2, waiting for transfers between devices, rows_of(): return lax.psum_scatter(term, 'seq', scatter_dimension=0, tiled=True)  73.7 us
    all_to_all x4, waiting for transfers between devices, spread(): lax.all_to_all(blocks, 'seq', 0, 0, tiled=True, axis_index_groups=runs if...  36.9 us
    all_gather x2, waiting for transfers between devices, whole(): return lax.all_gather(rows, 'seq', axis=0, tiled=True)  35.6 us
    ppermute x36, starting transfers between devices, flip(): return lax.ppermute(value, axis, [(i, i ^ bit) for i in range(count)])  26.5 us
    pallas_call x1, Pallas kernels, backward_scan(): pl.pallas_call(functools.partial(backward_kernel, half, 2, taps), grid=(m...  24.4 us
    all_to_all x4, starting transfers between devices, spread(): lax.all_to_all(blocks, 'seq', 0, 0, tiled=True, axis_index_groups=runs if...  18.9 us
  transfers between devices with their start and end apart: 44, of which 21 were waited for; matrix products, arithmetic and copies ran while one was open for 23% of the time, Pallas kernels for 11%

profile of v2, /device:TPU:0, one launch (start us, length us, event | category | flops | bytes accessed | tf_op | source)
XLA Modules:
  0.0 656.2 jit_solution(14562020891287925866)
XLA Ops:
  10.0 7.3 %all-to-all-start = ((bf16[8,64,768]{2,1,0:T(8,128)(2,1)}), bf16[8,64,768]{2,1,0:T(8,128)(2,1)S(1)}, u32[]{:S(2)}, u32[]{:S(2)}) async-start(bf16[8,64,768]{2,1,0:T(8,128)(2,1)} %constant_dynamic-slice_fusion.6), calls=%async_computation | async-start | bytes 1572864 | tf_op jit(solution)/shard_map/all_to_all | solution.py:75
  19.3 18.1 %all-to-all-done = bf16[8,64,768]{2,1,0:T(8,128)(2,1)S(1)} async-done(((bf16[8,64,768]{2,1,0:T(8,128)(2,1)}), bf16[8,64,768]{2,1,0:T(8,128)(2,1)S(1)}, u32[]{:S(2)}, u32[]{:S(2)}) %all-to-all-start) | async-done | bytes 786464 | tf_op jit(solution)/shard_map/all_to_all | solution.py:75
  37.5 3.6 all-to-all-start.1
  42.6 18.7 %all-to-all-done.1 = bf16[8,64,768]{2,1,0:T(8,128)(2,1)S(1)} async-done(((bf16[8,64,768]{2,1,0:T(8,128)(2,1)}), bf16[8,64,768]{2,1,0:T(8,128)(2,1)S(1)}, u32[]{:S(2)}, u32[]{:S(2)}) %all-to-all-start.1) | async-done | bytes 786464 | tf_op jit(solution)/shard_map/all_to_all | solution.py:75
  76.2 3.4 collective-permute-done.7
  90.4 3.5 fusion.1
  100.0 3.6 fusion.35.z_ref
  115.3 3.8 copy.146
  125.4 16.7 %shard_map.352 = (f32[2048,384]{1,0:T(8,128)}, f32[16,128,384]{2,1,0:T(8,128)}, f32[128,384]{1,0:T(8,128)}, bf16[2048,384]{1,0:T(8,128)(2,1)}, f32[4,8,64,768]{3,2,1,0:T(8,128)}, /*index=5*/f32[8,2048]{1,0:T(8,128)}) custom-call(s32[2]{0:T(128)} %pad_add_fusion.place_ref, f32[2048,384]{1,0:T(8,128)} %multiply_add_fusion.conv_ref, f32[2048,384]{1,0:T(8,128)} %fusion.35.z_ref, ...), custom_call_target="tpu_custom_call" | custom-call | tf_op jit(solution)/shard_map/pallas_call | solution.py:223
  150.6 12.2 %shard_map.353 = (f32[2048,384]{1,0:T(8,128)}, bf16[2048,384]{1,0:T(8,128)(2,1)}, bf16[2048,768]{1,0:T(8,128)(2,1)}, f32[1,384]{1,0:T(1,128)}) custom-call(s32[2]{0:T(128)} %pad_add_fusion.place_ref, bf16[2048,768]{1,0:T(8,128)(2,1)} %bitcast.153, f32[8,2048]{1,0:T(8,128)} %pad_maximum_fusion.8.norm_ref, f32[2048,384]{1,0:T(8,128)} %fusion.35.z_ref, ...), custom_call_target="tpu_custom_call" | custom-call | tf_op jit(solution)/shard_map/pallas_call | solution.py:299
  176.0 24.4 %shard_map.354 = (bf16[2048,384]{1,0:T(8,128)(2,1)}, f32[256,2048]{1,0:T(8,128)}, f32[16,2048]{1,0:T(8,128)}, f32[128,384]{1,0:T(8,128)}, f32[8,384]{1,0:T(8,128)}, /*index=5*/f32[8,384]{1,0:T(8,128)}) custom-call(f32[2048,384]{1,0:T(8,128)} %get-tuple-element.42.grad_ref, f32[2048,384]{1,0:T(8,128)} %multiply_add_fusion.conv_ref, ...), custom_call_target="tpu_custom_call" | custom-call | tf_op jit(solution)/shard_map/pallas_call | solution.py:470
  211.6 11.9 %collective-permute-done.17 = f32[64,2048]{1,0:T(8,128)} collective-permute-done((f32[64,2048]{1,0:T(8,128)}, f32[64,2048]{1,0:T(8,128)}, u32[]{:S(2)}, u32[]{:S(2)}) %collective-permute-start.17) | collective-permute-done | bytes 524320 | tf_op jit(solution)/shard_map/ppermute | solution.py:34
  228.6 4.5 fusion.10
  233.2 7.4 %reduce-scatter.7.cloned.1.call-done = f32[96,768]{1,0:T(8,128)} async-done(((f32[768,768]{1,0:T(8,128)}), f32[96,768]{1,0:T(8,128)}) %reduce-scatter.7.cloned.1.call-update) | async-done | bytes 294928 | tf_op jit(solution)/shard_map/reduce_scatter | solution.py:727
  242.3 66.3 %reduce-scatter.9.cloned.1.call-done = f32[96,454]{1,0:T(8,128)} async-done(((f32[768,454]{1,0:T(8,128)}), f32[96,454]{1,0:T(8,128)}) %reduce-scatter.9.cloned.1.call-update) | async-done | bytes 174352 | tf_op jit(solution)/shard_map/reduce_scatter | solution.py:727
  313.7 5.6 fusion.2
  329.6 3.3 bitcast_add_fusion
  336.8 9.0 %collective-permute-done.12 = bf16[8,64,768]{2,1,0:T(8,128)(2,1)} collective-permute-done((bf16[8,64,768]{2,1,0:T(8,128)(2,1)}, bf16[8,64,768]{2,1,0:T(8,128)(2,1)}, u32[]{:S(2)}, u32[]{:S(2)}) %collective-permute-start.12) | collective-permute-done | bytes 786464 | tf_op jit(solution)/shard_map/ppermute | solution.py:34
  345.8 16.5 %collective-permute-done.19 = bf16[8,64,768]{2,1,0:T(8,128)(2,1)} collective-permute-done((bf16[8,64,768]{2,1,0:T(8,128)(2,1)}, bf16[8,64,768]{2,1,0:T(8,128)(2,1)}, u32[]{:S(2)}, u32[]{:S(2)}) %collective-permute-start.19) | collective-permute-done | bytes 786464 | tf_op jit(solution)/shard_map/ppermute | solution.py:34
  362.3 4.8 fusion.22
  367.1 4.3 all-to-all-start.2
  374.9 3.9 fusion.31
  378.8 35.6 %all-gather.5.cloned.1.call-done = f32[768,454]{1,0:T(8,128)} async-done(((f32[96,454]{1,0:T(8,128)}), f32[768,454]{1,0:T(8,128)}) %all-gather.5.cloned.1.call-update) | async-done | bytes 1394704 | tf_op jit(solution)/shard_map/all_gather | solution.py:822
  414.4 5.4 convolution_add_fusion
  419.8 3.8 all-to-all-start.3
  464.2 10.6 %collective-permute-done.14 = bf16[8,64,768]{2,1,0:T(8,128)(2,1)} collective-permute-done((bf16[8,64,768]{2,1,0:T(8,128)(2,1)}, bf16[8,64,768]{2,1,0:T(8,128)(2,1)}, u32[]{:S(2)}, u32[]{:S(2)}) %collective-permute-start.14) | collective-permute-done | bytes 786464 | tf_op jit(solution)/shard_map/ppermute | solution.py:34
  474.8 16.8 %collective-permute-done.21 = bf16[8,64,768]{2,1,0:T(8,128)(2,1)} collective-permute-done((bf16[8,64,768]{2,1,0:T(8,128)(2,1)S(1)}, bf16[8,64,768]{2,1,0:T(8,128)(2,1)}, u32[]{:S(2)}, u32[]{:S(2)}) %collective-permute-start.21) | collective-permute-done | bytes 786464 | tf_op jit(solution)/shard_map/ppermute | solution.py:34
  494.8 22.1 %collective-permute-done.31 = f32[384,768]{1,0:T(8,128)} collective-permute-done((f32[384,768]{1,0:T(8,128)}, f32[384,768]{1,0:T(8,128)}, u32[]{:S(2)}, u32[]{:S(2)}) %collective-permute-start.31) | collective-permute-done | bytes 1179680 | tf_op jit(solution)/shard_map/ppermute | solution.py:34
  524.0 13.5 %collective-permute-done.34 = f32[384,768]{1,0:T(8,128)S(1)} collective-permute-done((f32[384,768]{1,0:T(8,128)}, f32[384,768]{1,0:T(8,128)S(1)}, u32[]{:S(2)}, u32[]{:S(2)}) %collective-permute-start.34) | collective-permute-done | bytes 1179680 | tf_op jit(solution)/shard_map/ppermute | solution.py:34
  544.3 3.4 copy.155
  549.4 46.7 %shard_map.355 = f32[96,768]{1,0:T(8,128)} custom-call(f32[768,768]{1,0:T(8,128)} %pad_maximum_fusion.1.gram_ref, bf16[96,768]{1,0:T(8,128)(2,1)} %fusion.51.pick_ref), custom_call_target="tpu_custom_call" | custom-call | tf_op jit(solution)/shard_map/pallas_call | solution.py:568
  597.8 46.6 %shard_map.356 = f32[96,768]{1,0:T(8,128)} custom-call(f32[768,768]{1,0:T(8,128)} %pad_maximum_fusion.2.gram_ref, bf16[96,768]{1,0:T(8,128)(2,1)} %fusion.51.pick_ref), custom_call_target="tpu_custom_call" | custom-call | tf_op jit(solution)/shard_map/pallas_call | solution.py:568
  (357 shorter events, 179.6 us)
Async XLA Ops:
  10.0 27.4 %all-to-all-start = ((bf16[8,64,768]{2,1,0:T(8,128)(2,1)}), bf16[8,64,768]{2,1,0:T(8,128)(2,1)S(1)}, u32[]{:S(2)}, u32[]{:S(2)}) async-start(bf16[8,64,768]{2,1,0:T(8,128)(2,1)} %constant_dynamic-slice_fusion.6), calls=%async_computation | async-start | bytes 1572864 | tf_op jit(solution)/shard_map/all_to_all | solution.py:75
  37.5 23.9 %all-to-all-start.1 = ((bf16[8,64,768]{2,1,0:T(8,128)(2,1)}), bf16[8,64,768]{2,1,0:T(8,128)(2,1)S(1)}, u32[]{:S(2)}, u32[]{:S(2)}) async-start(bf16[8,64,768]{2,1,0:T(8,128)(2,1)} %constant_dynamic-slice_fusion.5), calls=%async_computation.1 | async-start | bytes 1572864 | tf_op jit(solution)/shard_map/all_to_all | solution.py:75
  41.0 199.6 %reduce-scatter.7.cloned.1.call-start = ((), (), s32[]{:S(2)}) async-start(), calls=%async_computation.8 | async-start | bytes 2654208 | tf_op jit(solution)/shard_map/reduce_scatter | solution.py:727
  41.1 33.8 %collective-permute-start.1 = (bf16[8,64,768]{2,1,0:T(8,128)(2,1)S(1)}, bf16[8,64,768]{2,1,0:T(8,128)(2,1)}, u32[]{:S(2)}, u32[]{:S(2)}) collective-permute-start(bf16[8,64,768]{2,1,0:T(8,128)(2,1)S(1)} %all-to-all-done), channel_id=1, source_target_pairs={{0,2},{1,3},{2,0},{3,1},{4,6},{5,7},{6,4},{7,5},{8,10},{9,11},{10,... | collective-permute-start | bytes 2359304 | tf_op jit(solution)/shard_map/ppermute | solution.py:34
  61.4 18.2 %collective-permute-start.7 = (bf16[8,64,768]{2,1,0:T(8,128)(2,1)S(1)}, bf16[8,64,768]{2,1,0:T(8,128)(2,1)}, u32[]{:S(2)}, u32[]{:S(2)}) collective-permute-start(bf16[8,64,768]{2,1,0:T(8,128)(2,1)S(1)} %all-to-all-done.1), channel_id=1, source_target_pairs={{0,2},{1,3},{2,0},{3,1},{4,6},{5,7},{6,4},{7,5},{8,10},{9,11},{10,... | collective-permute-start | bytes 2359304 | tf_op jit(solution)/shard_map/ppermute | solution.py:34
  62.9 16.7 %collective-permute-start.6 = (bf16[8,64,768]{2,1,0:T(8,128)(2,1)S(1)}, bf16[8,64,768]{2,1,0:T(8,128)(2,1)}, u32[]{:S(2)}, u32[]{:S(2)}) collective-permute-start(bf16[8,64,768]{2,1,0:T(8,128)(2,1)S(1)} %all-to-all-done.1), channel_id=1, source_target_pairs={{0,1},{1,0},{2,3},{3,2},{4,5},{5,4},{6,7},{7,6},{8,9},{9,8},{10,11... | collective-permute-start | bytes 2359304 | tf_op jit(solution)/shard_map/ppermute | solution.py:34
  66.6 15.7 %collective-permute-start = (bf16[8,64,768]{2,1,0:T(8,128)(2,1)S(1)}, bf16[8,64,768]{2,1,0:T(8,128)(2,1)}, u32[]{:S(2)}, u32[]{:S(2)}) collective-permute-start(bf16[8,64,768]{2,1,0:T(8,128)(2,1)S(1)} %all-to-all-done), channel_id=1, source_target_pairs={{0,1},{1,0},{2,3},{3,2},{4,5},{5,4},{6,7},{7,6},{8,9},{9,8},{10,11... | collective-permute-start | bytes 2359304 | tf_op jit(solution)/shard_map/ppermute | solution.py:34
  79.6 24.0 %collective-permute-start.8 = (bf16[8,64,768]{2,1,0:T(8,128)(2,1)}, bf16[8,64,768]{2,1,0:T(8,128)(2,1)}, u32[]{:S(2)}, u32[]{:S(2)}) collective-permute-start(bf16[8,64,768]{2,1,0:T(8,128)(2,1)} %collective-permute-done.7), channel_id=1, source_target_pairs={{0,1},{1,0},{2,3},{3,2},{4,5},{5,4},{6,7},{7,6},{8,9},{9,8},{10,11... | collective-permute-start | bytes 2359304 | tf_op jit(solution)/shard_map/ppermute | solution.py:34
  96.4 17.9 %collective-permute-start.4 = (bf16[64,2048]{1,0:T(8,128)(2,1)S(1)}, bf16[64,2048]{1,0:T(8,128)(2,1)}, u32[]{:S(2)}, u32[]{:S(2)}) collective-permute-start(bf16[64,2048]{1,0:T(8,128)(2,1)S(1)} %get-tuple-element.183), channel_id=1, source_target_pairs={{0,2},{1,3},{2,0},{3,1},{4,6},{5,7},{6,4},{7,5},{8,10},{9,11},{10,... | collective-permute-start | bytes 786440 | tf_op jit(solution)/shard_map/ppermute | solution.py:34
  97.9 21.2 %collective-permute-start.3 = (bf16[64,2048]{1,0:T(8,128)(2,1)S(1)}, bf16[64,2048]{1,0:T(8,128)(2,1)}, u32[]{:S(2)}, u32[]{:S(2)}) collective-permute-start(bf16[64,2048]{1,0:T(8,128)(2,1)S(1)} %get-tuple-element.183), channel_id=1, source_target_pairs={{0,1},{1,0},{2,3},{3,2},{4,5},{5,4},{6,7},{7,6},{8,9},{9,8},{10,11... | collective-permute-start | bytes 786440 | tf_op jit(solution)/shard_map/ppermute | solution.py:34
  172.0 136.6 %reduce-scatter.9.cloned.1.call-start = ((), (), s32[]{:S(2)}) async-start(), calls=%async_computation.9 | async-start | bytes 1769472 | tf_op jit(solution)/shard_map/reduce_scatter | solution.py:727
  209.1 14.3 %collective-permute-start.17 = (f32[64,2048]{1,0:T(8,128)}, f32[64,2048]{1,0:T(8,128)}, u32[]{:S(2)}, u32[]{:S(2)}) collective-permute-start(f32[64,2048]{1,0:T(8,128)} %dynamic-slice_bitcast_fusion.4), channel_id=1, source_target_pairs={{0,2},{1,3},{2,0},{3,1},{4,6},{5,7},{6,4},{7,5},{8,10},{9,11},{10,... | collective-permute-start | bytes 1572872 | tf_op jit(solution)/shard_map/ppermute | solution.py:34
  233.2 141.7 %all-gather.3.cloned.1.call-start = ((), (), s32[]{:S(2)}) async-start(), calls=%async_computation.6 | async-start | bytes 2654208 | tf_op jit(solution)/shard_map/all_gather | solution.py:822
  311.1 103.3 %all-gather.5.cloned.1.call-start = ((), (), s32[]{:S(2)}) async-start(), calls=%async_computation.7 | async-start | bytes 1769472 | tf_op jit(solution)/shard_map/all_gather | solution.py:822
  313.6 10.0 %collective-permute-start.11 = (f32[2,8,64,768]{3,2,1,0:T(8,128)S(1)}, f32[2,8,64,768]{3,2,1,0:T(8,128)S(1)}, u32[]{:S(2)}, u32[]{:S(2)}) collective-permute-start(f32[2,8,64,768]{3,2,1,0:T(8,128)S(1)} %dynamic-slice_bitcast_fusion), channel_id=1, source_target_pairs={{0,1},{1,0},{2,3},{3,2},{4,5},{5,4},{6,7},{7,6},{8,9},{9,8},{10,11... | collective-permute-start | bytes 9437192 | tf_op jit(solution)/shard_map/ppermute | solution.py:34
  325.2 20.7 %collective-permute-start.12 = (bf16[8,64,768]{2,1,0:T(8,128)(2,1)}, bf16[8,64,768]{2,1,0:T(8,128)(2,1)}, u32[]{:S(2)}, u32[]{:S(2)}) collective-permute-start(bf16[8,64,768]{2,1,0:T(8,128)(2,1)} %fusion.33), channel_id=1, source_target_pairs={{0,2},{1,3},{2,0},{3,1},{4,6},{5,7},{6,4},{7,5},{8,10},{9,11},{10,... | collective-permute-start | bytes 2359304 | tf_op jit(solution)/shard_map/ppermute | solution.py:34
  333.9 28.4 %collective-permute-start.19 = (bf16[8,64,768]{2,1,0:T(8,128)(2,1)}, bf16[8,64,768]{2,1,0:T(8,128)(2,1)}, u32[]{:S(2)}, u32[]{:S(2)}) collective-permute-start(bf16[8,64,768]{2,1,0:T(8,128)(2,1)} %fusion.34), channel_id=1, source_target_pairs={{0,2},{1,3},{2,0},{3,1},{4,6},{5,7},{6,4},{7,5},{8,10},{9,11},{10,... | collective-permute-start | bytes 2359304 | tf_op jit(solution)/shard_map/ppermute | solution.py:34
  367.1 52.7 %all-to-all-start.2 = ((bf16[8,64,768]{2,1,0:T(8,128)(2,1)}), bf16[8,64,768]{2,1,0:T(8,128)(2,1)}, u32[]{:S(2)}, u32[]{:S(2)}) async-start(bf16[8,64,768]{2,1,0:T(8,128)(2,1)} %get-tuple-element.187), calls=%async_computation.2 | async-start | bytes 1572864 | tf_op jit(solution)/shard_map/all_to_all | solution.py:75
  371.6 59.7 %collective-permute-start.23 = (f32[768]{0:T(1024)S(1)}, f32[768]{0:T(1024)S(1)}, u32[]{:S(2)}, u32[]{:S(2)}) collective-permute-start(f32[768]{0:T(1024)S(1)} %get-tuple-element.148), channel_id=1, source_target_pairs={{0,1},{1,0},{2,3},{3,2},{4,5},{5,4},{6,7},{7,6},{8,9},{9,8},{10,11... | collective-permute-start | bytes 9224 | tf_op jit(solution)/shard_map/ppermute | solution.py:34
  419.8 35.2 %all-to-all-start.3 = ((bf16[8,64,768]{2,1,0:T(8,128)(2,1)}), bf16[8,64,768]{2,1,0:T(8,128)(2,1)S(1)}, u32[]{:S(2)}, u32[]{:S(2)}) async-start(bf16[8,64,768]{2,1,0:T(8,128)(2,1)} %fusion.21), calls=%async_computation.3 | async-start | bytes 1572864 | tf_op jit(solution)/shard_map/all_to_all | solution.py:75
  426.1 29.9 %collective-permute-start.30 = (f32[384,768]{1,0:T(8,128)}, f32[384,768]{1,0:T(8,128)}, u32[]{:S(2)}, u32[]{:S(2)}) collective-permute-start(f32[384,768]{1,0:T(8,128)} %dynamic-slice_bitcast_fusion.2), channel_id=1, source_target_pairs={{0,1},{1,0},{2,3},{3,2},{4,5},{5,4},{6,7},{7,6},{8,9},{9,8},{10,11... | collective-permute-start | bytes 3538952 | tf_op jit(solution)/shard_map/ppermute | solution.py:34
  430.7 29.2 %collective-permute-start.33 = (f32[384,768]{1,0:T(8,128)}, f32[384,768]{1,0:T(8,128)}, u32[]{:S(2)}, u32[]{:S(2)}) collective-permute-start(f32[384,768]{1,0:T(8,128)} %dynamic-slice_bitcast_fusion.1), channel_id=1, source_target_pairs={{0,1},{1,0},{2,3},{3,2},{4,5},{5,4},{6,7},{7,6},{8,9},{9,8},{10,11... | collective-permute-start | bytes 3538952 | tf_op jit(solution)/shard_map/ppermute | solution.py:34
  454.0 20.8 %collective-permute-start.14 = (bf16[8,64,768]{2,1,0:T(8,128)(2,1)}, bf16[8,64,768]{2,1,0:T(8,128)(2,1)}, u32[]{:S(2)}, u32[]{:S(2)}) collective-permute-start(bf16[8,64,768]{2,1,0:T(8,128)(2,1)} %all-to-all-done.2), channel_id=1, source_target_pairs={{0,2},{1,3},{2,0},{3,1},{4,6},{5,7},{6,4},{7,5},{8,10},{9,11},{10,... | collective-permute-start | bytes 2359304 | tf_op jit(solution)/shard_map/ppermute | solution.py:34
  454.9 63.7 %collective-permute-start.13 = (bf16[8,64,768]{2,1,0:T(8,128)(2,1)}, bf16[8,64,768]{2,1,0:T(8,128)(2,1)}, u32[]{:S(2)}, u32[]{:S(2)}) collective-permute-start(bf16[8,64,768]{2,1,0:T(8,128)(2,1)} %all-to-all-done.2), channel_id=1, source_target_pairs={{0,1},{1,0},{2,3},{3,2},{4,5},{5,4},{6,7},{7,6},{8,9},{9,8},{10,11... | collective-permute-start | bytes 2359304 | tf_op jit(solution)/shard_map/ppermute | solution.py:34
  455.0 36.7 %collective-permute-start.21 = (bf16[8,64,768]{2,1,0:T(8,128)(2,1)S(1)}, bf16[8,64,768]{2,1,0:T(8,128)(2,1)}, u32[]{:S(2)}, u32[]{:S(2)}) collective-permute-start(bf16[8,64,768]{2,1,0:T(8,128)(2,1)S(1)} %all-to-all-done.3), channel_id=1, source_target_pairs={{0,2},{1,3},{2,0},{3,1},{4,6},{5,7},{6,4},{7,5},{8,10},{9,11},{10,... | collective-permute-start | bytes 2359304 | tf_op jit(solution)/shard_map/ppermute | solution.py:34
  458.9 58.0 %collective-permute-start.31 = (f32[384,768]{1,0:T(8,128)}, f32[384,768]{1,0:T(8,128)}, u32[]{:S(2)}, u32[]{:S(2)}) collective-permute-start(f32[384,768]{1,0:T(8,128)} %bitcast_add_fusion.5), channel_id=1, source_target_pairs={{0,2},{1,3},{2,0},{3,1},{4,6},{5,7},{6,4},{7,5},{8,10},{9,11},{10,... | collective-permute-start | bytes 3538952 | tf_op jit(solution)/shard_map/ppermute | solution.py:34
  462.3 75.2 %collective-permute-start.34 = (f32[384,768]{1,0:T(8,128)}, f32[384,768]{1,0:T(8,128)S(1)}, u32[]{:S(2)}, u32[]{:S(2)}) collective-permute-start(f32[384,768]{1,0:T(8,128)} %bitcast_add_fusion.4), channel_id=1, source_target_pairs={{0,2},{1,3},{2,0},{3,1},{4,6},{5,7},{6,4},{7,5},{8,10},{9,11},{10,... | collective-permute-start | bytes 3538952 | tf_op jit(solution)/shard_map/ppermute | solution.py:34
  474.8 46.8 %collective-permute-start.20 = (bf16[8,64,768]{2,1,0:T(8,128)(2,1)S(1)}, bf16[8,64,768]{2,1,0:T(8,128)(2,1)S(1)}, u32[]{:S(2)}, u32[]{:S(2)}) collective-permute-start(bf16[8,64,768]{2,1,0:T(8,128)(2,1)S(1)} %all-to-all-done.3), channel_id=1, source_target_pairs={{0,1},{1,0},{2,3},{3,2},{4,5},{5,4},{6,7},{7,6},{8,9},{9,8},{10,11... | collective-permute-start | bytes 2359304 | tf_op jit(solution)/shard_map/ppermute | solution.py:34
  491.6 30.2 %collective-permute-start.15 = (bf16[8,64,768]{2,1,0:T(8,128)(2,1)}, bf16[8,64,768]{2,1,0:T(8,128)(2,1)}, u32[]{:S(2)}, u32[]{:S(2)}) collective-permute-start(bf16[8,64,768]{2,1,0:T(8,128)(2,1)} %collective-permute-done.14), channel_id=1, source_target_pairs={{0,1},{1,0},{2,3},{3,2},{4,5},{5,4},{6,7},{7,6},{8,9},{9,8},{10,11... | collective-permute-start | bytes 2359304 | tf_op jit(solution)/shard_map/ppermute | solution.py:34
  516.9 24.7 %collective-permute-start.22 = (bf16[8,64,768]{2,1,0:T(8,128)(2,1)}, bf16[8,64,768]{2,1,0:T(8,128)(2,1)S(1)}, u32[]{:S(2)}, u32[]{:S(2)}) collective-permute-start(bf16[8,64,768]{2,1,0:T(8,128)(2,1)} %collective-permute-done.21), channel_id=1, source_target_pairs={{0,1},{1,0},{2,3},{3,2},{4,5},{5,4},{6,7},{7,6},{8,9},{9,8},{10,11... | collective-permute-start | bytes 2359304 | tf_op jit(solution)/shard_map/ppermute | solution.py:34
  518.7 29.0 %collective-permute-start.32 = (f32[384,768]{1,0:T(8,128)S(1)}, f32[384,768]{1,0:T(8,128)S(1)}, u32[]{:S(2)}, u32[]{:S(2)}) collective-permute-start(f32[384,768]{1,0:T(8,128)S(1)} %add.369), channel_id=1, source_target_pairs={{0,1},{1,0},{2,3},{3,2},{4,5},{5,4},{6,7},{7,6},{8,9},{9,8},{10,11... | collective-permute-start | bytes 3538952 | tf_op jit(solution)/shard_map/ppermute | solution.py:34
  539.0 57.1 %collective-permute-start.35 = (f32[384,768]{1,0:T(8,128)S(1)}, f32[384,768]{1,0:T(8,128)S(1)}, u32[]{:S(2)}, u32[]{:S(2)}) collective-permute-start(f32[384,768]{1,0:T(8,128)S(1)} %add.373), channel_id=1, source_target_pairs={{0,1},{1,0},{2,3},{3,2},{4,5},{5,4},{6,7},{7,6},{8,9},{9,8},{10,11... | collective-permute-start | bytes 3538952 | tf_op jit(solution)/shard_map/ppermute | solution.py:34
  (83 other events, 1094.8 us)
Sparse Core Ops, SparseCore 0:
  172.1 68.4 reduce-scatter.6
  244.6 63.9 reduce-scatter.8
  311.6 50.8 all-gather.2
  364.8 49.6 all-gather.4
